TPU v7x, 256 devices: a whole 4x4x8 slice. The times are simulated.
256 devices in a mesh: region: 8 (over x, core), member: 32 (over z, y).
Axes of the slice: x: 4, y: 4, z: 8, core: 2. Of those that a mesh axis runs over, the one named last changes fastest.
Arguments:
- background_trajectories: bfloat16 [256, 6, 65536], P('member', None, 'region'), may hold values from -6 to 6
- sensor_spread_matrix: bfloat16 [256, 114688], P('member', 'region'), may hold values from -2 to 2
- departure_vector: float32 [114688], P('region'), may hold values from -6 to 6
- inverse_error_variance: float32 [114688], P('region'), may hold values from 0.3 to 3
- edge_tile_handoff: int32 [2, 32], P(None, 'region'), may hold values from 0 to 55
- measurement_tile_table: int32 [512, 16], P(('region', 'member')), may hold values from 0 to 63
- distance_damping: float32 [512, 16], P(('region', 'member')), may hold values from 0.1 to 1
- active_tile_tally: int32 [512], P(('region', 'member')), may hold values from 1 to 16, as said below
Outputs:
- analysis: bfloat16 [256, 6, 65536], P('member', None, 'region')
Inputs may be any that keep to these rules, and one draw needn't show every extreme that they name: `edge_tile_handoff`: indices of a region's own observation blocks. `measurement_tile_table`: indices into the region's extended set; entries at positions at or past active_tile_tally are unused. `active_tile_tally`: some column block uses all 16 slots.
All inputs are finite; a program needn't handle non-finite values. Where the computation divides by a largest or mean magnitude, that divisor is 1e-20 or more.
Results may differ from a plain program's by a relative error of at most 0.0075.
Values may be sent and summed in bfloat16 or wider, within the bound.
No kernel may reach another device: no remote copies, remote signals or barrier semaphores. Data moves between devices by JAX's collectives and lax.ppermute only.
A program may use at most 128 MiB of HBM per device.

v0:
```python
import jax
import jax.numpy as jnp
from jax import lax
from jax.sharding import PartitionSpec as P

READINGS_BUNDLE = 256
COMMON_STENCIL = 128
NSIT = 3


def shifted(value, axis, by):
    length = lax.axis_size(axis)
    pairs = [(i, i + by) for i in range(length) if 0 <= i + by < length]
    return lax.ppermute(value, axis, pairs)


def update_coefficients(cross_product_accumulated, projected_innovation, background_copies):
    unit_diagonal = jnp.eye(background_copies, dtype=jnp.float32)
    linear_equations = unit_diagonal + cross_product_accumulated / (background_copies - 1.0)
    bound = jnp.max(jnp.sum(jnp.abs(linear_equations), axis=-1), axis=-1)
    root_iter = linear_equations / bound[:, None, None]
    inverse_root = jnp.broadcast_to(unit_diagonal, linear_equations.shape)
    for iteration in range(NSIT):
        factor = 1.5 * unit_diagonal - 0.5 * jnp.matmul(
            inverse_root, root_iter, precision=lax.Precision.HIGHEST
        )
        if iteration + 1 < NSIT:
            root_iter = jnp.matmul(root_iter, factor, precision=lax.Precision.HIGHEST)
        inverse_root = jnp.matmul(factor, inverse_root, precision=lax.Precision.HIGHEST)
    dispersion_factor = inverse_root / jnp.sqrt(bound)[:, None, None]
    scalar_product = jnp.matmul(
        dispersion_factor, projected_innovation[:, :, None], precision=lax.Precision.HIGHEST
    )
    centre_increment = jnp.matmul(
        dispersion_factor, scalar_product, precision=lax.Precision.HIGHEST
    )[:, :, 0] / (background_copies - 1.0)
    return (dispersion_factor + centre_increment[:, :, None]).astype(jnp.bfloat16)


def on_device(
    background_trajectories,
    sensor_spread_matrix,
    departure_vector,
    inverse_error_variance,
    edge_tile_handoff,
    measurement_tile_table,
    distance_damping,
    active_tile_tally,
):
    local_trajectories = sensor_spread_matrix.shape[0]
    background_copies = local_trajectories * lax.axis_size("member")
    own_blocks = departure_vector.shape[0] // READINGS_BUNDLE
    strip_groups = measurement_tile_table.shape[0]
    ens_blocks = sensor_spread_matrix.reshape(local_trajectories, own_blocks, READINGS_BUNDLE)
    val_blocks = departure_vector.reshape(own_blocks, READINGS_BUNDLE)
    wgt_blocks = inverse_error_variance.reshape(own_blocks, READINGS_BUNDLE)
    to_next = edge_tile_handoff[0]
    to_prev = edge_tile_handoff[1]
    from_left = (
        shifted(jnp.take(ens_blocks, to_next, axis=1), "region", 1),
        shifted(jnp.take(val_blocks, to_next, axis=0).astype(jnp.bfloat16), "region", 1).astype(
            jnp.float32
        ),
        shifted(jnp.take(wgt_blocks, to_next, axis=0).astype(jnp.bfloat16), "region", 1).astype(
            jnp.float32
        ),
    )
    from_right = (
        shifted(jnp.take(ens_blocks, to_prev, axis=1), "region", -1),
        shifted(jnp.take(val_blocks, to_prev, axis=0).astype(jnp.bfloat16), "region", -1).astype(
            jnp.float32
        ),
        shifted(jnp.take(wgt_blocks, to_prev, axis=0).astype(jnp.bfloat16), "region", -1).astype(
            jnp.float32
        ),
    )
    ext_ens = jnp.concatenate([from_left[0], ens_blocks, from_right[0]], axis=1)
    ext_val = jnp.concatenate([from_left[1], val_blocks, from_right[1]], axis=0)
    ext_wgt = jnp.concatenate([from_left[2], wgt_blocks, from_right[2]], axis=0)
    weighted_val = ext_wgt * ext_val
    gathered = lax.all_gather(ext_ens, "member", axis=0, tiled=True)

    def one_block(entries):
        listed, local_weights, used = entries

        def add_entry(position, carry):
            gram_acc, vector_acc = carry
            block = listed[position]
            pert_block = lax.dynamic_index_in_dim(gathered, block, 1, keepdims=False)
            block_wgt = lax.dynamic_index_in_dim(ext_wgt, block, 0, keepdims=False)
            block_val = lax.dynamic_index_in_dim(weighted_val, block, 0, keepdims=False)
            pert_wide = pert_block.astype(jnp.float32)
            scaled = (pert_wide * block_wgt[None, :]).astype(jnp.bfloat16)
            term = lax.dot_general(
                pert_block, scaled, (((1,), (1,)), ((), ())), preferred_element_type=jnp.float32
            )
            gram_acc = gram_acc + local_weights[position] * term
            vector_acc = vector_acc + local_weights[position] * jnp.dot(
                pert_wide, block_val, precision=lax.Precision.HIGHEST
            )
            return (gram_acc, vector_acc)

        return lax.fori_loop(
            0,
            used,
            add_entry,
            (
                jnp.zeros((background_copies, background_copies), jnp.float32),
                jnp.zeros((background_copies,), jnp.float32),
            ),
        )

    cross_product_accumulated, projected_innovation = lax.map(
        one_block, (measurement_tile_table, distance_damping, active_tile_tally)
    )
    combination_matrix = update_coefficients(
        cross_product_accumulated, projected_innovation, background_copies
    )
    horizontal_mesh = lax.all_to_all(
        background_trajectories, "member", split_axis=2, concat_axis=0, tiled=True
    )
    height_strata = horizontal_mesh.shape[1]
    average_centre = jnp.sum(horizontal_mesh, axis=0, dtype=jnp.float32) / background_copies
    pert = (
        (horizontal_mesh - average_centre)
        .astype(jnp.bfloat16)
        .reshape(background_copies, height_strata, strip_groups, COMMON_STENCIL)
    )
    mixed = jnp.einsum(
        "ilcq,cij->jlcq", pert, combination_matrix, preferred_element_type=jnp.float32
    )
    returned_output = (
        average_centre.reshape(height_strata, strip_groups, COMMON_STENCIL) + mixed
    ).astype(jnp.bfloat16)
    returned_output = returned_output.reshape(
        background_copies, height_strata, strip_groups * COMMON_STENCIL
    )
    return lax.all_to_all(returned_output, "member", split_axis=0, concat_axis=2, tiled=True)


def solution(mesh):
    placed = (
        P("member", None, "region"),
        P("member", "region"),
        P("region"),
        P("region"),
        P(None, "region"),
        P(("region", "member"), None),
        P(("region", "member"), None),
        P(("region", "member")),
    )
    return jax.shard_map(
        on_device,
        mesh=mesh,
        in_specs=placed,
        out_specs=P("member", None, "region"),
        check_vma=False,
    )
```

profile of v0, /device:TPU:13, one launch (start us, length us, event | category | flops | bytes accessed | tf_op | source)
XLA Modules:
  0.0 414.6 jit_solution(8642611954827483138)
XLA Ops:
  7.3 1.5 gather_fusion.1
  8.9 2.6 collective-permute-start.1
  11.5 1.5 gather_fusion
  13.0 3.0 collective-permute-start
  16.9 1.7 pad_maximum_fusion
  18.6 13.5 %copy.34 = bf16[8,6,8192]{0,1,2:T(8,128)(2,1)} copy(bf16[8,6,8192]{2,0,1:T(8,128)(2,1)} %param.16) | data formatting | bytes 1572864 | tf_op args[0]
  32.1 18.3 %reshape.156 = bf16[32,2,6144]{2,1,0:T(2,128)(2,1)} reshape(bf16[8192,6,8]{2,1,0:T(8,128)(2,1)} %bitcast.110) | data formatting | bytes 1572864
  50.4 11.1 %all-to-all-start = ((bf16[32,2,6144]{2,1,0:T(2,128)(2,1)}), bf16[32,2,6144]{2,1,0:T(2,128)(2,1)S(1)}, u32[]{:S(2)}, u32[]{:S(2)}) async-start(bf16[32,2,6144]{2,1,0:T(2,128)(2,1)} %reshape.156), calls=%async_computation | async-start | bytes 1572864 | tf_op jit(solution)/shard_map/all_to_all | solution.py:119
  62.8 3.7 collective-permute-start.5
  67.7 2.9 collective-permute-start.4
  70.6 1.9 collective-permute-start.3
  72.6 3.6 collective-permute-start.2
  77.8 5.3 %all-to-all-done = bf16[32,2,6144]{2,1,0:T(2,128)(2,1)S(1)} async-done(((bf16[32,2,6144]{2,1,0:T(2,128)(2,1)}), bf16[32,2,6144]{2,1,0:T(2,128)(2,1)S(1)}, u32[]{:S(2)}, u32[]{:S(2)}) %all-to-all-start) | async-done | bytes 786464 | tf_op jit(solution)/shard_map/all_to_all | solution.py:119
  83.1 16.5 %reshape.157 = bf16[8192,6,8]{2,1,0:T(8,128)(2,1)} reshape(bf16[32,2,6144]{2,1,0:T(2,128)(2,1)S(1)} %all-to-all-done) | data formatting | bytes 1572864
  99.6 15.3 %copy.36 = f32[8,6,32,256]{3,0,2,1:T(8,128)S(1)} copy(bf16[8,6,32,256]{0,1,3,2:T(8,128)(2,1)} %bitcast.109) | data formatting | bytes 2359296 | tf_op jit(solution)/shard_map/convert_element_type | solution.py:123
  116.5 17.4 %convert_reduce_fusion = f32[6,8192]{0,1:T(8,128)} fusion(bf16[8192,6,8]{2,1,0:T(8,128)(2,1)} %reshape.157), kind=kLoop, calls=%fused_computation.27 | loop fusion | flops 737280 | bytes 983040 | tf_op jit(solution)/shard_map/reduce_sum | solution.py:123
  133.9 2.6 reduce_sum.27
  136.6 176.8 %while.25 = (s32[]{:T(128)}, f32[2,256,256]{2,1,0:T(8,128)S(1)}, f32[2,256]{1,0:T(2,128)S(1)}, s32[2]{0:T(128)S(1)}, s32[2,16]{1,0:T(2,128)S(1)}, /*index=5*/f32...) while((s32[]{:T(128)}, f32[2,256,256]{2,1,0:T(8,128)S(1)}, ...), condition=%wide.region_5.8_spmd, body=%wide.region_2.7_spmd.sunk | while | flops 34669064 | bytes 1718554 | solution.py:113
  137.3 119.0 %while.26 = (s32[]{:T(128)}, f32[256,256]{1,0:T(8,128)S(1)}, f32[256]{0:T(256)S(1)}, s32[]{:T(128)}, f32[16]{0:T(128)S(1)}, /*index=5*/s32[16]{0:T(128)S(1)}, bf...) while((s32[]{:T(128)}, f32[256,256]{1,0:T(8,128)S(1)}, ...), condition=%wide.region_4.6_spmd, body=%wide.region_3.5_spmd.sunk | while | flops 34669064 | bytes 928489 | solution.py:103
  141.4 1.9 fusion.68
  143.3 1.1 fusion.69
  149.3 1.9 fusion.68
  157.2 1.9 fusion.68
  165.1 1.9 fusion.68
  173.0 1.9 fusion.68
  180.9 1.9 fusion.68
  188.8 1.9 fusion.68
  190.7 1.1 fusion.69
  196.7 1.9 fusion.68
  204.5 1.9 fusion.68
  212.4 1.9 fusion.68
  220.3 1.9 fusion.68
  228.2 1.9 fusion.68
  230.1 1.1 fusion.69
  236.1 1.9 fusion.68
  244.0 1.9 fusion.68
  251.9 1.9 fusion.68
  253.8 1.1 fusion.69
  257.1 55.9 %while.26 = (s32[]{:T(128)}, f32[256,256]{1,0:T(8,128)S(1)}, f32[256]{0:T(256)S(1)}, s32[]{:T(128)}, f32[16]{0:T(128)S(1)}, /*index=5*/s32[16]{0:T(128)S(1)}, bf...) while((s32[]{:T(128)}, f32[256,256]{1,0:T(8,128)S(1)}, ...), condition=%wide.region_4.6_spmd, body=%wide.region_3.5_spmd.sunk | while | flops 34669064 | bytes 928489 | solution.py:103
  261.3 1.9 fusion.68
  263.2 1.1 fusion.69
  269.2 1.9 fusion.68
  277.0 1.9 fusion.68
  284.9 1.9 fusion.68
  292.8 1.9 fusion.68
  300.7 1.9 fusion.68
  308.6 1.9 fusion.68
  321.8 84.9 %all_to_all.27 = bf16[256,6,256]{2,1,0:T(8,128)(2,1)S(1)} all-to-all(bf16[256,6,256]{2,1,0:T(8,128)(2,1)S(1)} %copy.39), channel_id=1, replica_groups=mesh['region'=8,'member'=32] {'member'}, dimensions={0} | all-to-all | bytes 1572864 | tf_op jit(solution)/shard_map/all_to_all | solution.py:138
  (189 shorter events, 83.3 us)
Async XLA Ops:
  6.5 130.0 %all-gather.2.cloned.1.call-start = ((), (), s32[]{:S(2)}) async-start(), calls=%async_computation.2 | async-start | bytes 8650752 | tf_op jit(solution)/shard_map/all_gather | solution.py:81
  8.9 7.1 %collective-permute-start.1 = (bf16[8,4,256]{2,0,1:T(8,128)(2,1)S(1)}, bf16[8,4,256]{2,0,1:T(8,128)(2,1)S(1)}, u32[]{:S(2)}, u32[]{:S(2)}) collective-permute-start(bf16[8,4,256]{2,0,1:T(8,128)(2,1)S(1)} %select_bitcast_fusion), channel_id=1, source_target_pairs={{32,0},{64,32},{96,64},{128,96},{160,128},{192,160},{224,192},{33,... | collective-permute-start | bytes 49160 | tf_op jit(solution)/shard_map/ppermute | solution.py:14
  13.0 3.8 collective-permute-start
  32.1 29.4 %copy-start.3 = (f32[14336]{0:T(1024)S(1)}, f32[14336]{0:T(1024)}, u32[]{:S(2)}) copy-start(f32[14336]{0:T(1024)} %param.18) | copy-start | bytes 172036
  32.1 30.0 %copy-start.4 = (f32[14336]{0:T(1024)S(1)}, f32[14336]{0:T(1024)}, u32[]{:S(2)}) copy-start(f32[14336]{0:T(1024)} %param.19) | copy-start | bytes 172036
  50.4 32.7 %all-to-all-start = ((bf16[32,2,6144]{2,1,0:T(2,128)(2,1)}), bf16[32,2,6144]{2,1,0:T(2,128)(2,1)S(1)}, u32[]{:S(2)}, u32[]{:S(2)}) async-start(bf16[32,2,6144]{2,1,0:T(2,128)(2,1)} %reshape.156), calls=%async_computation | async-start | bytes 1572864 | tf_op jit(solution)/shard_map/all_to_all | solution.py:119
  62.8 14.9 %collective-permute-start.5 = (bf16[4,256]{1,0:T(4,128)(2,1)S(1)}, bf16[4,256]{1,0:T(4,128)(2,1)S(1)}, u32[]{:S(2)}, u32[]{:S(2)}) collective-permute-start(bf16[4,256]{1,0:T(4,128)(2,1)S(1)} %get-tuple-element.152), channel_id=1, source_target_pairs={{32,0},{64,32},{96,64},{128,96},{160,128},{192,160},{224,192},{33,... | collective-permute-start | bytes 6152 | tf_op jit(solution)/shard_map/ppermute | solution.py:14
  67.7 10.0 %collective-permute-start.4 = (bf16[4,256]{1,0:T(4,128)(2,1)S(1)}, bf16[4,256]{1,0:T(4,128)(2,1)S(1)}, u32[]{:S(2)}, u32[]{:S(2)}) collective-permute-start(bf16[4,256]{1,0:T(4,128)(2,1)S(1)} %get-tuple-element.150), channel_id=1, source_target_pairs={{0,32},{32,64},{64,96},{96,128},{128,160},{160,192},{192,224},{1,3... | collective-permute-start | bytes 6152 | tf_op jit(solution)/shard_map/ppermute | solution.py:14
  70.6 7.1 %collective-permute-start.3 = (bf16[4,256]{1,0:T(4,128)(2,1)S(1)}, bf16[4,256]{1,0:T(4,128)(2,1)S(1)}, u32[]{:S(2)}, u32[]{:S(2)}) collective-permute-start(bf16[4,256]{1,0:T(4,128)(2,1)S(1)} %get-tuple-element.153), channel_id=1, source_target_pairs={{32,0},{64,32},{96,64},{128,96},{160,128},{192,160},{224,192},{33,... | collective-permute-start | bytes 6152 | tf_op jit(solution)/shard_map/ppermute | solution.py:14
  72.6 5.2 %collective-permute-start.2 = (bf16[4,256]{1,0:T(4,128)(2,1)S(1)}, bf16[4,256]{1,0:T(4,128)(2,1)S(1)}, u32[]{:S(2)}, u32[]{:S(2)}) collective-permute-start(bf16[4,256]{1,0:T(4,128)(2,1)S(1)} %get-tuple-element.151), channel_id=1, source_target_pairs={{0,32},{32,64},{64,96},{96,128},{128,160},{160,192},{192,224},{1,3... | collective-permute-start | bytes 6152 | tf_op jit(solution)/shard_map/ppermute | solution.py:14
  133.9 2.7 copy-start.2
  133.9 2.7 copy-start.5
  133.9 2.7 copy-start.6
  133.9 2.7 copy-start.7
  136.6 176.8 %copy-start.1 = (f32[256,256]{1,0:T(8,128)S(1)}, f32[256,256]{1,0:T(8,128)}, u32[]{:S(2)}) copy-start(f32[256,256]{1,0:T(8,128)} %fusion.27) | copy-start | bytes 786436
  136.6 177.1 %copy-start = (f32[256,256]{1,0:T(8,128)S(1)}, f32[256,256]{1,0:T(8,128)}, u32[]{:S(2)}) copy-start(f32[256,256]{1,0:T(8,128)} %fusion.28) | copy-start | bytes 786436
Sparse Core Ops, SparseCore 0:
  18.7 108.9 all-gather.1
where the time goes:
time: 419 us; the launch traced here: 415 us
  local copies, waits for them, and re-layouts  104 us (25%)
  blocking collectives  84.9 us (20%)
  matrix products  72.7 us (17%)
  loops' own time  63.1 us (15%)
  other arithmetic  41.5 us (10%)
  starting transfers between devices  28.9 us (7%)
  between operations  13.8 us (3%)
  waiting for transfers between devices  6.2 us (1%)
    all_to_all x1, blocking collectives, on_device(): lax.all_to_all(returned_output, 'member', split_axis=0, concat_axis=2, ti...  84.9 us
    another operation x2, loops' own time, one_block(): lax.fori_loop(0, used, add_entry, (jnp.zeros((background_copies, backgrou...  62.8 us
    unnamed x19, local copies, waits for them, and re-layouts  48.3 us
    dot_general x22, matrix products, add_entry(): lax.dot_general(pert_block, scaled, (((1,), (1,)), ((), ())), preferred_e...  41.8 us
    dot_general x22, matrix products, add_entry(): jnp.dot(pert_wide, block_val, precision=lax.Precision.HIGHEST)  23.9 us
    reduce_sum x2, other arithmetic, on_device(): jnp.sum(horizontal_mesh, axis=0, dtype=jnp.float32) / background_copies  19.9 us
    ppermute x6, starting transfers between devices, shifted(): return lax.ppermute(value, axis, pairs)  17.7 us
    add x22, other arithmetic, add_entry(): vector_acc + local_weights[position] * jnp.dot(pert_wide, block_val, prec...  17 us
  transfers between devices with their start and end apart: 8, of which 2 were waited for; matrix products, arithmetic and copies ran while one was open for 22% of the time, Pallas kernels for 0%

commit v1 on v0

v1 whole, which is shorter than its diff:
```python
import jax
import jax.numpy as jnp
from jax import lax
from jax.experimental import pallas as pl
from jax.experimental.pallas import tpu as pltpu
from jax.sharding import PartitionSpec as P

F32 = jnp.float32
BF16 = jnp.bfloat16
MEMBERS = 256
PEERS = 32
OWN = 8
LEVELS = 6
OBS = 256
HANDED = 4
HOME = 56
EXT = 64
COLS = 256
MAXL = 16
VMEM_BYTES = 48 * 1024 * 1024
WHOLE = pl.BlockSpec(memory_space=pltpu.VMEM)
SCALARS = pl.BlockSpec(memory_space=pltpu.SMEM)
PARAMS = pltpu.CompilerParams(vmem_limit_bytes=VMEM_BYTES)


def iota(shape, dim):
    return lax.broadcasted_iota(jnp.int32, shape, dim)


def one_hot(shape, column_of_row):
    hit = iota(shape, 1) == column_of_row(iota(shape, 0))
    return jnp.where(hit, 1.0, 0.0).astype(BF16)


def dot(a, b):
    return jnp.dot(a, b, preferred_element_type=F32)


def split(a):
    high = a.astype(BF16)
    return high, (a - high.astype(F32)).astype(BF16)


def product(a, b):
    return dot(a[0], b[0]) + (dot(a[0], b[1]) + dot(a[1], b[0]))


def rounded(a):
    return a.astype(BF16).astype(F32)


def pick_kernel(chosen, ens, val, wgt, to_next, to_prev):
    row = iota((OWN, OBS), 0)
    for side, out in ((0, to_next), (1, to_prev)):
        for k in range(HANDED):
            block = chosen[side, k]
            at = pl.ds(pl.multiple_of(block * OBS, OBS), OBS)
            pert = ens[:, at].astype(F32)
            w = jnp.concatenate(
                [wgt[pl.ds(2 * block, 1), :], wgt[pl.ds(2 * block + 1, 1), :]], axis=1
            )
            v = jnp.concatenate(
                [val[pl.ds(2 * block, 1), :], val[pl.ds(2 * block + 1, 1), :]], axis=1
            )
            w_high, v_high = rounded(w), rounded(v)
            tail = jnp.where(
                row == 0,
                w_high,
                jnp.where(
                    row == 1,
                    w - w_high,
                    jnp.where(row == 2, v_high, jnp.where(row == 3, v - v_high, 0.0)),
                ),
            )
            out[:, k * OBS : (k + 1) * OBS] = jnp.concatenate([pert, tail], axis=0).astype(BF16)


def pack_kernel(fields, ens, left, right, out, wide):
    wide[:, LEVELS:, :] = jnp.zeros((OWN, 8 - LEVELS, wide.shape[2]), F32)
    wide[:, :LEVELS, :] = fields[...].astype(F32)
    order = one_hot((LEVELS * OWN, 64), lambda r: (r & 7) * 8 + (r >> 3))
    for peer in range(PEERS):
        rows = wide[:, :, peer * COLS : (peer + 1) * COLS].reshape(64, COLS).astype(BF16)
        out[peer, : LEVELS * OWN, :] = dot(order, rows).astype(BF16)
        if peer < 2:
            source, start = left, peer * 2 * OBS
        elif peer < PEERS - 2:
            source, start = ens, (peer - 2) * 2 * OBS
        else:
            source, start = right, (peer - PEERS + 2) * 2 * OBS
        first = source[:OWN, start : start + OBS].astype(F32)
        second = source[:OWN, start + OBS : start + 2 * OBS].astype(F32)
        out[peer, LEVELS * OWN :, :] = jnp.concatenate([first, second], axis=0).astype(BF16)


def gram_kernel(me, table, damping, tally, pert, val, wgt, left, right, out):
    wide = pert[...].astype(F32)
    lane = iota((128, 128), 1)
    row = iota((128, 128), 0) & 3
    block_of_lane = iota((1, 128), 1) - 64
    top, low = [], []
    for half in range(2):
        block = 2 * me[0] + half
        own = jnp.clip(block - HANDED, 0, HOME - 1)
        w = jnp.concatenate(
            [wgt[pl.ds(2 * own, 1), :], wgt[pl.ds(2 * own + 1, 1), :]], axis=1
        )
        v = jnp.concatenate(
            [val[pl.ds(2 * own, 1), :], val[pl.ds(2 * own + 1, 1), :]], axis=1
        )
        from_left = jnp.clip(block, 0, HANDED - 1)
        from_right = jnp.clip(block - HANDED - HOME, 0, HANDED - 1)
        at_left = left[:, pl.ds(pl.multiple_of(from_left * OBS, OBS), OBS)].astype(F32)
        at_right = right[:, pl.ds(pl.multiple_of(from_right * OBS, OBS), OBS)].astype(F32)
        is_left = block < HANDED
        is_right = block >= HANDED + HOME
        w = jnp.where(
            is_left,
            at_left[8:9] + at_left[9:10],
            jnp.where(is_right, at_right[8:9] + at_right[9:10], w),
        )
        v = jnp.where(
            is_left,
            at_left[10:11] + at_left[11:12],
            jnp.where(is_right, at_right[10:11] + at_right[11:12], v),
        )
        y = wide[:, half * OWN : (half + 1) * OWN, :].reshape(MEMBERS, OBS)
        scaled = (y * w).astype(BF16)
        gram = lax.dot_general(
            y.astype(BF16), scaled, (((1,), (1,)), ((), ())), preferred_element_type=F32
        )
        vector = jnp.sum(y * (w * v), axis=1, keepdims=True)
        vector_high = rounded(vector)
        vector_low = vector - vector_high
        coeff = jnp.zeros((1, 128), F32)
        for position in range(MAXL):
            used = jnp.where(position < tally[half], damping[half, position], 0.0)
            coeff = coeff + jnp.where(block_of_lane == table[half, position], used, 0.0)
        coeff_high = rounded(coeff)
        extra = jnp.where(row == 0, coeff_high, jnp.where(row == 1, coeff - coeff_high, 0.0))
        for place, column in enumerate(
            (vector_high[:128], vector_low[:128], vector_high[128:], vector_low[128:])
        ):
            extra = jnp.where(lane == place, column, extra)
        top.append(gram[:128, :])
        low.append(jnp.concatenate([gram[128:, 128:], extra], axis=1))
    stacked = jnp.concatenate(top + low, axis=0).astype(BF16)
    order = one_hot(
        (512, 512), lambda r: ((r >> 3) & 1) * 256 + ((r >> 2) & 1) * 128 + (r >> 4) * 4 + (r & 3)
    )
    out[...] = dot(order, stacked).reshape(PEERS, 16, 256).astype(BF16)


def combine_kernel(entries, out):
    x = entries[...].astype(F32).reshape(512, 256).astype(BF16)
    coeffs = x[:, 128:]
    row = iota((512, 512), 0)
    column = iota((512, 512), 1)
    same = ((row ^ column) & 11) == 0
    spread_out = jnp.where(
        iota((128, 512), 0) - 64
        == 2 * (iota((128, 512), 1) >> 4) + ((iota((128, 512), 1) >> 2) & 1),
        1.0,
        0.0,
    ).astype(BF16)
    total = None
    for part in range(2):
        take = one_hot((512, 512), lambda r: (r & ~15) + 8 + (r & 4) + part)
        wide = dot(dot(take, coeffs).astype(BF16), spread_out)
        term = dot(jnp.where(same, wide, 0.0).astype(BF16), x)
        total = term if total is None else total + term
    tail = total[:, 128:]
    both = tail + pltpu.roll(tail, 127, 1)
    high = rounded(both)
    low = pltpu.roll(both - high, 1, 1)
    lane = iota((512, 128), 1)
    has_vector = ((iota((512, 128), 0) & 8) != 0) & (lane < 4)
    tail = jnp.where(has_vector, jnp.where((lane & 1) == 0, high, low), tail)
    out[...] = (
        jnp.concatenate([total[:, :128], tail], axis=1).reshape(PEERS, 16, 256).astype(BF16)
    )


def centre_kernel(fields, pert, centre):
    wide = fields[...].astype(F32)
    for level in range(LEVELS):
        x = wide[:, level * OWN : (level + 1) * OWN, :].reshape(MEMBERS, COLS)
        mean = jnp.sum(x, axis=0, keepdims=True) / MEMBERS
        away = (x - mean).astype(BF16)
        for half in range(2):
            at = slice(level * 128, (level + 1) * 128)
            pert[half, :, at] = away[:, half * 128 : (half + 1) * 128]
            centre[half, :, at] = jnp.broadcast_to(
                mean[:, half * 128 : (half + 1) * 128], (8, 128)
            )


def mix_kernel(entries, pert, centre, out):
    x = entries[...].astype(F32).reshape(512, 256).astype(BF16)
    order = one_hot(
        (512, 512), lambda r: ((r & 127) >> 2) * 16 + (r >> 8) * 8 + ((r >> 7) & 1) * 4 + (r & 3)
    )
    sorted_rows = dot(order, x)
    eye = jnp.where(iota((256, 256), 0) == iota((256, 256), 1), 1.0, 0.0)
    vectors, bounds, a1 = [], [], []
    for half in range(2):
        top = sorted_rows[half * 128 : (half + 1) * 128]
        low = sorted_rows[256 + half * 128 : 256 + (half + 1) * 128]
        gram = jnp.concatenate(
            [top, jnp.concatenate([top[:, 128:].T, low[:, :128]], axis=1)], axis=0
        )
        vectors.append(
            jnp.concatenate(
                [low[:, 128:129] + low[:, 129:130], low[:, 130:131] + low[:, 131:132]], axis=0
            )
        )
        system = eye + gram * (1.0 / (MEMBERS - 1.0))
        sums = jnp.sum(jnp.abs(system), axis=1, keepdims=True)
        bound = jnp.max(sums, axis=0, keepdims=True)
        bounds.append(bound)
        a1.append(system / bound)
    s1 = [split(a) for a in a1]
    a2 = [product(s, s) for s in s1]
    s2 = [split(a) for a in a2]
    a3 = [product(s, t) for s, t in zip(s2, s1)]
    a4 = [product(s, s) for s in s2]
    z2 = [
        2.25 * eye - 2.4375 * a + 1.6875 * b - 0.5625 * c + 0.0625 * d
        for a, b, c, d in zip(a1, a2, a3, a4)
    ]
    t2 = [split(z) for z in z2]
    az = [split(product(s, t)) for s, t in zip(s1, t2)]
    zz = [split(product(t, t)) for t in t2]
    z3 = [1.5 * z - 0.5 * product(a, b) for z, a, b in zip(z2, az, zz)]
    for half in range(2):
        spread = z3[half] / jnp.sqrt(bounds[half])
        inner = jnp.sum(spread * vectors[half], axis=0, keepdims=True)
        shift = jnp.sum(spread * inner, axis=1, keepdims=True) / (MEMBERS - 1.0)
        mixing = (spread + shift).T.astype(BF16)
        result = dot(mixing, pert[half]) + centre[half][:1]
        for pair in range(LEVELS // 2):
            rows = jnp.concatenate(
                [
                    result[:, level * 128 : (level + 1) * 128].reshape(PEERS, OWN, 128)
                    for level in (2 * pair, 2 * pair + 1)
                ],
                axis=1,
            )
            out[:, pair * 16 : (pair + 1) * 16, half * 128 : (half + 1) * 128] = rows.astype(BF16)


def unpack_kernel(parts, out):
    order = one_hot((64, LEVELS * OWN), lambda r: (r & 7) * 8 + (r >> 3))
    for peer in range(PEERS):
        rows = dot(order, parts[peer]).reshape(OWN, 8, COLS)
        out[:, :, peer * COLS : (peer + 1) * COLS] = rows[:, :LEVELS].astype(BF16)


def shifted(value, by):
    length = lax.axis_size("region")
    pairs = [(i, i + by) for i in range(length) if 0 <= i + by < length]
    return lax.ppermute(value, "region", pairs)


def exchange(value):
    return lax.all_to_all(value, "member", split_axis=0, concat_axis=0, tiled=True)


def shape(*dims, dtype=BF16):
    return jax.ShapeDtypeStruct(dims, dtype)


def on_device(
    background_trajectories,
    sensor_spread_matrix,
    departure_vector,
    inverse_error_variance,
    edge_tile_handoff,
    measurement_tile_table,
    distance_damping,
    active_tile_tally,
):
    val = departure_vector.reshape(2 * HOME, 128)
    wgt = inverse_error_variance.reshape(2 * HOME, 128)
    me = lax.axis_index("member").reshape(1)

    to_next, to_prev = pl.pallas_call(
        pick_kernel,
        out_shape=(shape(16, HANDED * OBS), shape(16, HANDED * OBS)),
        in_specs=[SCALARS, WHOLE, WHOLE, WHOLE],
        out_specs=(WHOLE, WHOLE),
        compiler_params=PARAMS,
        name="pick",
    )(edge_tile_handoff, sensor_spread_matrix, val, wgt)
    left = shifted(to_next, 1)
    right = shifted(to_prev, -1)

    packed = pl.pallas_call(
        pack_kernel,
        out_shape=shape(PEERS, 64, COLS),
        in_specs=[WHOLE] * 4,
        out_specs=WHOLE,
        scratch_shapes=[pltpu.VMEM((OWN, 8, PEERS * COLS), F32)],
        compiler_params=PARAMS,
        name="pack",
    )(background_trajectories, sensor_spread_matrix, left, right)
    gathered = exchange(packed)

    grams = pl.pallas_call(
        gram_kernel,
        grid=(1,),
        out_shape=shape(PEERS, 16, 256),
        in_specs=[SCALARS] * 4
        + [pl.BlockSpec((PEERS, 16, COLS), lambda i: (0, 3, 0))]
        + [WHOLE] * 4,
        out_specs=pl.BlockSpec((PEERS, 16, 256), lambda i: (0, 0, 0)),
        compiler_params=PARAMS,
        name="gram",
    )(
        me,
        measurement_tile_table,
        distance_damping,
        active_tile_tally,
        gathered,
        val,
        wgt,
        left,
        right,
    )
    entries = exchange(grams)

    pert, centre = pl.pallas_call(
        centre_kernel,
        grid=(1,),
        out_shape=(shape(2, MEMBERS, LEVELS * 128), shape(2, 8, LEVELS * 128, dtype=F32)),
        in_specs=[pl.BlockSpec((PEERS, LEVELS * OWN, COLS), lambda i: (0, 0, 0))],
        out_specs=(
            pl.BlockSpec((2, MEMBERS, LEVELS * 128), lambda i: (0, 0, 0)),
            pl.BlockSpec((2, 8, LEVELS * 128), lambda i: (0, 0, 0)),
        ),
        compiler_params=PARAMS,
        name="centre",
    )(gathered)

    sums = pl.pallas_call(
        combine_kernel,
        out_shape=shape(PEERS, 16, 256),
        in_specs=[WHOLE],
        out_specs=WHOLE,
        compiler_params=PARAMS,
        name="combine",
    )(entries)
    systems = exchange(sums)

    mixed = pl.pallas_call(
        mix_kernel,
        out_shape=shape(PEERS, LEVELS * OWN, COLS),
        in_specs=[WHOLE] * 3,
        out_specs=WHOLE,
        compiler_params=PARAMS,
        name="mix",
    )(systems, pert, centre)
    returned = exchange(mixed)

    return pl.pallas_call(
        unpack_kernel,
        out_shape=shape(OWN, LEVELS, PEERS * COLS),
        in_specs=[WHOLE],
        out_specs=WHOLE,
        compiler_params=PARAMS,
        name="unpack",
    )(returned)


def solution(mesh):
    placed = (
        P("member", None, "region"),
        P("member", "region"),
        P("region"),
        P("region"),
        P(None, "region"),
        P(("region", "member"), None),
        P(("region", "member"), None),
        P(("region", "member")),
    )
    return jax.shard_map(
        on_device,
        mesh=mesh,
        in_specs=placed,
        out_specs=P("member", None, "region"),
        check_vma=False,
    )
```

time: 419 us -> 122 us (0.29)
  the two profiles are of different devices: /device:TPU:13 before, /device:TPU:2 now
where the time goes in v1:
time: 122 us
  blocking collectives  44.3 us (36%)
  waiting for transfers between devices  41 us (34%)
  starting transfers between devices  21.2 us (17%)
  Pallas kernels  9.08 us (7%)
  local copies, waits for them, and re-layouts  6.18 us (5%)
    all_to_all x2, blocking collectives, exchange(): lax.all_to_all(value, 'member', split_axis=0, concat_axis=0, tiled=True)  44.3 us
    all_to_all x2, waiting for transfers between devices, exchange(): lax.all_to_all(value, 'member', split_axis=0, concat_axis=0, tiled=True)  41 us
    all_to_all x2, starting transfers between devices, exchange(): lax.all_to_all(value, 'member', split_axis=0, concat_axis=0, tiled=True)  15.5 us
    ppermute x2, starting transfers between devices, shifted(): return lax.ppermute(value, 'region', pairs)  5.69 us
    unnamed x21, local copies, waits for them, and re-layouts  4.86 us
    pallas_call x1, Pallas kernels, on_device(): pl.pallas_call(mix_kernel, out_shape=shape(PEERS, LEVELS * OWN, COLS), in...  2.88 us
  transfers between devices with their start and end apart: 4, of which 2 were waited for; matrix products, arithmetic and copies ran while one was open for 1% of the time, Pallas kernels for 0%

profile of v1, /device:TPU:2, one launch (start us, length us, event | category | flops | bytes accessed | tf_op | source)
XLA Modules:
  0.0 121.9 jit_solution(3218638194482240099)
XLA Ops:
  0.0 0.0 copy-start.6
  0.0 0.7 copy-done.6
  0.7 0.0 copy-start
  0.7 0.9 copy-done
  1.6 0.0 copy-start.2
  1.6 0.8 copy-done.2
  2.4 0.0 copy-start.4
  2.4 0.8 copy-done.4
  3.3 0.6 pick.1
  3.9 1.9 %collective-permute-start = (bf16[16,1024]{1,0:T(8,128)(2,1)S(1)}, bf16[16,1024]{1,0:T(8,128)(2,1)S(1)}, u32[]{:S(2)}, u32[]{:S(2)}) collective-permute-start(bf16[16,1024]{1,0:T(8,128)(2,1)S(1)} %get-tuple-element.9), channel_id=1, source_target_pairs={{0,32},{32,64},{64,96},{96,128},{128,160},{160,192},{192,224},{1,3... | collective-permute-start | bytes 98312 | tf_op jit(solution)/shard_map/ppermute | solution.py:262
  5.8 0.0 copy-start.1
  5.8 3.8 %collective-permute-start.1 = (bf16[16,1024]{1,0:T(8,128)(2,1)S(1)}, bf16[16,1024]{1,0:T(8,128)(2,1)S(1)}, u32[]{:S(2)}, u32[]{:S(2)}) collective-permute-start(bf16[16,1024]{1,0:T(8,128)(2,1)S(1)} %get-tuple-element.10), channel_id=1, source_target_pairs={{32,0},{64,32},{96,64},{128,96},{160,128},{192,160},{224,192},{33,... | collective-permute-start | bytes 98312 | tf_op jit(solution)/shard_map/ppermute | solution.py:262
  9.6 1.6 %copy.9.fields = bf16[8,6,8192]{2,1,0:T(8,128)(2,1)S(1)} copy(bf16[8,6,8192]{2,0,1:T(8,128)(2,1)} %param.8) | data formatting | bytes 1572864 | tf_op args[0]
  11.2 0.0 collective-permute-done.left
  11.2 0.0 collective-permute-done.1.right
  11.2 0.0 copy-done.1
  11.2 1.5 %pack.1 = bf16[32,64,256]{2,1,0:T(8,128)(2,1)} custom-call(bf16[8,6,8192]{2,1,0:T(8,128)(2,1)S(1)} %copy.9.fields, bf16[8,14336]{1,0:T(8,128)(2,1)S(1)} %copy-done.1, bf16[16,1024]{1,0:T(8,128)(2,1)S(1)} %collective-permute-done.left, bf16[16,1024]{1,0:T(8,128)(2,1)S(1)} %collective-permute-done.1.right), custom_call_target="tpu_custom_call" | custom-call | tf_op jit(solution)/shard_map/pack/pallas_call | solution.py:298
  12.7 0.0 copy-start.3
  12.7 0.0 copy-start.5
  12.7 11.6 %all-to-all-start = ((bf16[32,64,256]{2,1,0:T(8,128)(2,1)}), bf16[32,64,256]{2,1,0:T(8,128)(2,1)S(1)}, u32[]{:S(2)}, u32[]{:S(2)}) async-start(bf16[32,64,256]{2,1,0:T(8,128)(2,1)} %pack.1), calls=%async_computation | async-start | bytes 2097152 | tf_op jit(solution)/shard_map/all_to_all | solution.py:266
  24.4 0.0 copy-start.8
  24.4 0.0 copy-start.7
  24.4 0.0 copy-start.9
  24.4 29.1 %all-to-all-done.pert.fields = bf16[32,64,256]{2,1,0:T(8,128)(2,1)S(1)} async-done(((bf16[32,64,256]{2,1,0:T(8,128)(2,1)}), bf16[32,64,256]{2,1,0:T(8,128)(2,1)S(1)}, u32[]{:S(2)}, u32[]{:S(2)}) %all-to-all-start) | async-done | bytes 1048608 | tf_op jit(solution)/shard_map/all_to_all | solution.py:266
  53.5 0.0 copy-done.3
  53.5 0.0 copy-done.5
  53.5 0.0 copy-done.8
  53.5 0.0 copy-done.7
  53.5 0.0 copy-done.9
  53.5 1.2 gram.1
  54.7 18.8 %all_to_all.20.entries = bf16[32,16,256]{2,1,0:T(8,128)(2,1)S(1)} all-to-all(bf16[32,16,256]{2,1,0:T(8,128)(2,1)S(1)} %gram.1), channel_id=1, replica_groups=mesh['region'=8,'member'=32] {'member'}, dimensions={0} | all-to-all | bytes 524288 | tf_op jit(solution)/shard_map/all_to_all | solution.py:266
  73.4 2.2 %combine.1 = bf16[32,16,256]{2,1,0:T(8,128)(2,1)} custom-call(bf16[32,16,256]{2,1,0:T(8,128)(2,1)S(1)} %all_to_all.20.entries), custom_call_target="tpu_custom_call" | custom-call | tf_op jit(solution)/shard_map/combine/pallas_call | solution.py:345
  75.6 3.9 %all-to-all-start.2 = ((bf16[32,16,256]{2,1,0:T(8,128)(2,1)}), bf16[32,16,256]{2,1,0:T(8,128)(2,1)S(1)}, u32[]{:S(2)}, u32[]{:S(2)}) async-start(bf16[32,16,256]{2,1,0:T(8,128)(2,1)} %combine.1), calls=%async_computation.2 | async-start | bytes 524288 | tf_op jit(solution)/shard_map/all_to_all | solution.py:266
  79.5 0.3 centre.1
  79.8 11.9 %all-to-all-done.2.entries = bf16[32,16,256]{2,1,0:T(8,128)(2,1)S(1)} async-done(((bf16[32,16,256]{2,1,0:T(8,128)(2,1)}), bf16[32,16,256]{2,1,0:T(8,128)(2,1)S(1)}, u32[]{:S(2)}, u32[]{:S(2)}) %all-to-all-start.2) | async-done | bytes 262176 | tf_op jit(solution)/shard_map/all_to_all | solution.py:266
  91.7 2.9 %mix.1 = bf16[32,48,256]{2,1,0:T(8,128)(2,1)S(1)} custom-call(bf16[32,16,256]{2,1,0:T(8,128)(2,1)S(1)} %all-to-all-done.2.entries, bf16[2,256,768]{2,1,0:T(8,128)(2,1)S(1)} %get-tuple-element.11.pert, f32[2,8,768]{2,1,0:T(8,128)S(1)} %get-tuple-element.12.centre), custom_call_target="tpu_custom_call" | custom-call | tf_op jit(solution)/shard_map/mix/pallas_call | solution.py:355
  94.6 25.5 %all_to_all.21.parts = bf16[32,48,256]{2,1,0:T(8,128)(2,1)S(1)} all-to-all(bf16[32,48,256]{2,1,0:T(8,128)(2,1)S(1)} %mix.1), channel_id=1, replica_groups=mesh['region'=8,'member'=32] {'member'}, dimensions={0} | all-to-all | bytes 1572864 | tf_op jit(solution)/shard_map/all_to_all | solution.py:266
  120.2 0.4 unpack.1
  120.6 1.3 %copy.10 = bf16[8,6,8192]{2,0,1:T(8,128)(2,1)} copy(bf16[8,6,8192]{2,1,0:T(8,128)(2,1)S(1)} %unpack.1) | data formatting | bytes 1572864 | tf_op jit(solution)/shard_map/unpack/pallas_call | solution.py:365
Async XLA Ops:
  0.0 0.7 copy-start.6
  0.7 0.9 copy-start
  1.6 0.8 copy-start.2
  2.4 0.8 copy-start.4
  3.9 7.3 %collective-permute-start = (bf16[16,1024]{1,0:T(8,128)(2,1)S(1)}, bf16[16,1024]{1,0:T(8,128)(2,1)S(1)}, u32[]{:S(2)}, u32[]{:S(2)}) collective-permute-start(bf16[16,1024]{1,0:T(8,128)(2,1)S(1)} %get-tuple-element.9), channel_id=1, source_target_pairs={{0,32},{32,64},{64,96},{96,128},{128,160},{160,192},{192,224},{1,3... | collective-permute-start | bytes 98312 | tf_op jit(solution)/shard_map/ppermute | solution.py:262
  5.8 5.4 %copy-start.1 = (bf16[8,14336]{1,0:T(8,128)(2,1)S(1)}, bf16[8,14336]{1,0:T(8,128)(2,1)}, u32[]{:S(2)}) copy-start(bf16[8,14336]{1,0:T(8,128)(2,1)} %ens.3) | copy-start | bytes 688132
  5.8 5.4 %collective-permute-start.1 = (bf16[16,1024]{1,0:T(8,128)(2,1)S(1)}, bf16[16,1024]{1,0:T(8,128)(2,1)S(1)}, u32[]{:S(2)}, u32[]{:S(2)}) collective-permute-start(bf16[16,1024]{1,0:T(8,128)(2,1)S(1)} %get-tuple-element.10), channel_id=1, source_target_pairs={{32,0},{64,32},{96,64},{128,96},{160,128},{192,160},{224,192},{33,... | collective-permute-start | bytes 98312 | tf_op jit(solution)/shard_map/ppermute | solution.py:262
  12.7 40.7 %copy-start.3 = (f32[14336]{0:T(1024)S(1)}, f32[14336]{0:T(1024)}, u32[]{:S(2)}) copy-start(f32[14336]{0:T(1024)} %param.10) | copy-start | bytes 172036
  12.7 40.7 %copy-start.5 = (f32[14336]{0:T(1024)S(1)}, f32[14336]{0:T(1024)}, u32[]{:S(2)}) copy-start(f32[14336]{0:T(1024)} %param.11) | copy-start | bytes 172036
  12.7 40.7 %all-to-all-start = ((bf16[32,64,256]{2,1,0:T(8,128)(2,1)}), bf16[32,64,256]{2,1,0:T(8,128)(2,1)S(1)}, u32[]{:S(2)}, u32[]{:S(2)}) async-start(bf16[32,64,256]{2,1,0:T(8,128)(2,1)} %pack.1), calls=%async_computation | async-start | bytes 2097152 | tf_op jit(solution)/shard_map/all_to_all | solution.py:266
  24.4 29.1 %copy-start.8 = (f32[2,16]{1,0:T(2,128)S(1)}, f32[2,16]{1,0:T(2,128)}, u32[]{:S(2)}) copy-start(f32[2,16]{1,0:T(2,128)} %damping.1) | copy-start | bytes 388
  24.4 29.1 %copy-start.7 = (s32[2,16]{1,0:T(2,128)S(1)}, s32[2,16]{1,0:T(2,128)}, u32[]{:S(2)}) copy-start(s32[2,16]{1,0:T(2,128)} %table.1) | copy-start | bytes 388
  24.4 29.1 %copy-start.9 = (s32[2]{0:T(128)S(1)}, s32[2]{0:T(128)}, u32[]{:S(2)}) copy-start(s32[2]{0:T(128)} %tally.1) | copy-start | bytes 28
  75.6 16.1 %all-to-all-start.2 = ((bf16[32,16,256]{2,1,0:T(8,128)(2,1)}), bf16[32,16,256]{2,1,0:T(8,128)(2,1)S(1)}, u32[]{:S(2)}, u32[]{:S(2)}) async-start(bf16[32,16,256]{2,1,0:T(8,128)(2,1)} %combine.1), calls=%async_computation.2 | async-start | bytes 524288 | tf_op jit(solution)/shard_map/all_to_all | solution.py:266

commit v2 on v1

v2 whole, which is shorter than its diff:
```python
import jax
import jax.numpy as jnp
from jax import lax
from jax.experimental import pallas as pl
from jax.experimental.pallas import tpu as pltpu
from jax.sharding import PartitionSpec as P

F32 = jnp.float32
BF16 = jnp.bfloat16
MEMBERS = 256
PEERS = 32
OWN = 8
LEVELS = 6
OBS = 256
HANDED = 4
HOME = 56
EXT = 64
COLS = 256
MAXL = 16
VMEM_BYTES = 48 * 1024 * 1024
WHOLE = pl.BlockSpec(memory_space=pltpu.VMEM)
ANY = pl.BlockSpec(memory_space=pl.ANY)
HBM = pl.BlockSpec(memory_space=pltpu.HBM)
SCALARS = pl.BlockSpec(memory_space=pltpu.SMEM)
SPLIT = True
PARAMS = pltpu.CompilerParams(vmem_limit_bytes=VMEM_BYTES)


def iota(shape, dim):
    return lax.broadcasted_iota(jnp.int32, shape, dim)


def one_hot(shape, column_of_row):
    hit = iota(shape, 1) == column_of_row(iota(shape, 0))
    return jnp.where(hit, 1.0, 0.0).astype(BF16)


def dot(a, b):
    return jnp.dot(a, b, preferred_element_type=F32)


def split(a):
    high = a.astype(BF16)
    return high, (a - high.astype(F32)).astype(BF16)


def product(a, b):
    return dot(a[0], b[0]) + (dot(a[0], b[1]) + dot(a[1], b[0]))


def rounded(a):
    return a.astype(BF16).astype(F32)


def in_flight(pairs, sems):
    copies = [pltpu.make_async_copy(*ends, sems.at[k]) for k, ends in enumerate(pairs)]
    for copy in copies:
        copy.start()
    return copies


def landed(copies):
    for copy in copies:
        copy.wait()


def wide_row(pair):
    return jnp.concatenate([pair[:1], pair[1:]], axis=1)


def pick_kernel(chosen, blocks, val, wgt, to_next, to_prev, vals, wgts, sems):
    pairs = []
    for side, out in ((0, to_next), (1, to_prev)):
        for k in range(HANDED):
            block = chosen[side, k]
            pairs += [
                (blocks.at[block], out.at[k]),
                (val.at[block], vals.at[side * HANDED + k]),
                (wgt.at[block], wgts.at[side * HANDED + k]),
            ]
    landed(in_flight(pairs, sems))
    row = iota((OWN, OBS), 0)
    for side, out in ((0, to_next), (1, to_prev)):
        for k in range(HANDED):
            w = wide_row(wgts[side * HANDED + k])
            v = wide_row(vals[side * HANDED + k])
            w_high, v_high = rounded(w), rounded(v)
            tail = jnp.where(row == 2, v_high, jnp.where(row == 3, v - v_high, 0.0))
            tail = jnp.where(row == 0, w_high, jnp.where(row == 1, w - w_high, tail))
            out[HANDED + k] = tail.astype(BF16)


def own_pairs(blocks, left, right, out, group):
    pairs = []
    for peer in range(PEERS):
        if peer < 2:
            source = left.at[pl.ds(2 * peer, 2)]
        elif peer < PEERS - 2:
            source = blocks.at[pl.ds(2 * peer - HANDED, 2)]
        else:
            source = right.at[pl.ds(2 * (peer - PEERS + 2), 2)]
        pairs.append((source, out.at[peer, pl.ds(group, 2)]))
    return pairs


def field_pairs(fields, out):
    return [
        (fields.at[:, :, pl.ds(peer * COLS, COLS)], out.at[peer, pl.ds(0, LEVELS)])
        for peer in range(PEERS)
    ]


def pack_both_kernel(fields, blocks, left, right, out, sems):
    pairs = field_pairs(fields, out) + own_pairs(blocks, left, right, out, LEVELS)
    landed(in_flight(pairs, sems))


def pack_blocks_kernel(blocks, left, right, out, sems):
    landed(in_flight(own_pairs(blocks, left, right, out, 0), sems))


def grams_of(me, table, damping, tally, val, wgt, left, right, pert):
    lane = iota((128, 128), 1)
    row = iota((128, 128), 0) & 3
    block_of_lane = iota((1, 128), 1) - 64
    top, low = [], []
    for half in range(2):
        block = 2 * me[0] + half
        own = jnp.clip(block - HANDED, 0, HOME - 1)
        w, v = wide_row(wgt[own]), wide_row(val[own])
        at_left = left[HANDED + jnp.clip(block, 0, HANDED - 1)].astype(F32)
        at_right = right[HANDED + jnp.clip(block - HANDED - HOME, 0, HANDED - 1)].astype(F32)
        is_left = block < HANDED
        is_right = block >= HANDED + HOME
        w = jnp.where(
            is_left,
            at_left[0:1] + at_left[1:2],
            jnp.where(is_right, at_right[0:1] + at_right[1:2], w),
        )
        v = jnp.where(
            is_left,
            at_left[2:3] + at_left[3:4],
            jnp.where(is_right, at_right[2:3] + at_right[3:4], v),
        )
        y = pert(half).astype(F32).reshape(MEMBERS, OBS)
        scaled = (y * w).astype(BF16)
        gram = lax.dot_general(
            y.astype(BF16), scaled, (((1,), (1,)), ((), ())), preferred_element_type=F32
        )
        vector = jnp.sum(y * (w * v), axis=1, keepdims=True)
        vector_high = rounded(vector)
        vector_low = vector - vector_high
        coeff = jnp.zeros((1, 128), F32)
        for position in range(MAXL):
            used = jnp.where(position < tally[half], damping[half, position], 0.0)
            coeff = coeff + jnp.where(block_of_lane == table[half, position], used, 0.0)
        coeff_high = rounded(coeff)
        extra = jnp.where(row == 0, coeff_high, jnp.where(row == 1, coeff - coeff_high, 0.0))
        for place, column in enumerate(
            (vector_high[:128], vector_low[:128], vector_high[128:], vector_low[128:])
        ):
            extra = jnp.where(lane == place, column, extra)
        top.append(gram[:128, :])
        low.append(jnp.concatenate([gram[128:, 128:], extra], axis=1))
    stacked = jnp.concatenate(top + low, axis=0).astype(BF16)
    order = one_hot(
        (512, 512), lambda r: ((r >> 3) & 1) * 256 + ((r >> 2) & 1) * 128 + (r >> 4) * 4 + (r & 3)
    )
    return dot(order, stacked).reshape(PEERS, 2, 8, 256).astype(BF16)


def gram_kernel(me, table, damping, tally, val, wgt, left, right, gathered, out):
    group = gathered.shape[1] - 2
    out[...] = grams_of(
        me, table, damping, tally, val, wgt, left, right, lambda half: gathered[:, group + half]
    )


def gram_and_pack_kernel(
    me, table, damping, tally, val, wgt, left, right, gathered, fields, out, grams, sems
):
    copies = in_flight(field_pairs(fields, out), sems)
    grams[...] = grams_of(
        me, table, damping, tally, val, wgt, left, right, lambda half: gathered[:, half]
    )
    last = pltpu.make_async_copy(grams, out.at[:, pl.ds(LEVELS, 2)], sems.at[PEERS])
    last.start()
    landed(copies)
    last.wait()


def combine_kernel(entries, out):
    group = entries.shape[1] - 2
    x = entries[:, group:].astype(F32).reshape(512, 256).astype(BF16)
    coeffs = x[:, 128:]
    row = iota((512, 512), 0)
    column = iota((512, 512), 1)
    same = ((row ^ column) & 11) == 0
    spread_out = jnp.where(
        iota((128, 512), 0) - 64
        == 2 * (iota((128, 512), 1) >> 4) + ((iota((128, 512), 1) >> 2) & 1),
        1.0,
        0.0,
    ).astype(BF16)
    total = None
    for part in range(2):
        take = one_hot((512, 512), lambda r: (r & ~15) + 8 + (r & 4) + part)
        wide = dot(dot(take, coeffs).astype(BF16), spread_out)
        term = dot(jnp.where(same, wide, 0.0).astype(BF16), x)
        total = term if total is None else total + term
    tail = total[:, 128:]
    both = tail + pltpu.roll(tail, 127, 1)
    high = rounded(both)
    low = pltpu.roll(both - high, 1, 1)
    lane = iota((512, 128), 1)
    has_vector = ((iota((512, 128), 0) & 8) != 0) & (lane < 4)
    tail = jnp.where(has_vector, jnp.where((lane & 1) == 0, high, low), tail)
    out[...] = (
        jnp.concatenate([total[:, :128], tail], axis=1).reshape(PEERS, 2, 8, 256).astype(BF16)
    )


def centre_kernel(fields, pert, centre):
    for level in range(LEVELS):
        x = fields[:, level].astype(F32).reshape(MEMBERS, COLS)
        mean = jnp.sum(x, axis=0, keepdims=True) / MEMBERS
        away = (x - mean).astype(BF16)
        for half in range(2):
            at = slice(level * 128, (level + 1) * 128)
            pert[half, :, at] = away[:, half * 128 : (half + 1) * 128]
            centre[half, :, at] = jnp.broadcast_to(
                mean[:, half * 128 : (half + 1) * 128], (8, 128)
            )


def mix_kernel(entries, pert, centre, out):
    x = entries[...].astype(F32).reshape(512, 256).astype(BF16)
    order = one_hot(
        (512, 512), lambda r: ((r & 127) >> 2) * 16 + (r >> 8) * 8 + ((r >> 7) & 1) * 4 + (r & 3)
    )
    sorted_rows = dot(order, x)
    eye = jnp.where(iota((256, 256), 0) == iota((256, 256), 1), 1.0, 0.0)
    vectors, bounds, a1 = [], [], []
    for half in range(2):
        top = sorted_rows[half * 128 : (half + 1) * 128]
        low = sorted_rows[256 + half * 128 : 256 + (half + 1) * 128]
        gram = jnp.concatenate(
            [top, jnp.concatenate([top[:, 128:].T, low[:, :128]], axis=1)], axis=0
        )
        vectors.append(
            jnp.concatenate(
                [low[:, 128:129] + low[:, 129:130], low[:, 130:131] + low[:, 131:132]], axis=0
            )
        )
        system = eye + gram * (1.0 / (MEMBERS - 1.0))
        sums = jnp.sum(jnp.abs(system), axis=1, keepdims=True)
        bound = jnp.max(sums, axis=0, keepdims=True)
        bounds.append(bound)
        a1.append(system / bound)
    s1 = [split(a) for a in a1]
    a2 = [product(s, s) for s in s1]
    s2 = [split(a) for a in a2]
    a3 = [product(s, t) for s, t in zip(s2, s1)]
    a4 = [product(s, s) for s in s2]
    z2 = [
        2.25 * eye - 2.4375 * a + 1.6875 * b - 0.5625 * c + 0.0625 * d
        for a, b, c, d in zip(a1, a2, a3, a4)
    ]
    t2 = [split(z) for z in z2]
    az = [split(product(s, t)) for s, t in zip(s1, t2)]
    zz = [split(product(t, t)) for t in t2]
    z3 = [1.5 * z - 0.5 * product(a, b) for z, a, b in zip(z2, az, zz)]
    for half in range(2):
        spread = z3[half] / jnp.sqrt(bounds[half])
        inner = jnp.sum(spread * vectors[half], axis=0, keepdims=True)
        shift = jnp.sum(spread * inner, axis=1, keepdims=True) / (MEMBERS - 1.0)
        mixing = (spread + shift).T.astype(BF16)
        result = dot(mixing, pert[half]) + centre[half][:1]
        for level in range(LEVELS):
            rows = result[:, level * 128 : (level + 1) * 128].reshape(PEERS, OWN, 128)
            out[:, level, :, half * 128 : (half + 1) * 128] = rows.astype(BF16)


def unpack_kernel(parts, out, sems):
    copies = [
        pltpu.make_async_copy(
            parts.at[peer], out.at[:, :, pl.ds(peer * COLS, COLS)], sems.at[peer]
        )
        for peer in range(PEERS)
    ]
    for copy in copies:
        copy.start()
    for copy in copies:
        copy.wait()


def shifted(value, by):
    length = lax.axis_size("region")
    pairs = [(i, i + by) for i in range(length) if 0 <= i + by < length]
    return lax.ppermute(value, "region", pairs)


def exchange(value):
    return lax.all_to_all(value, "member", split_axis=0, concat_axis=0, tiled=True)


def shape(*dims, dtype=BF16):
    return jax.ShapeDtypeStruct(dims, dtype)


def on_device(
    background_trajectories,
    sensor_spread_matrix,
    departure_vector,
    inverse_error_variance,
    edge_tile_handoff,
    measurement_tile_table,
    distance_damping,
    active_tile_tally,
):
    val = departure_vector.reshape(HOME, 2, 128)
    wgt = inverse_error_variance.reshape(HOME, 2, 128)
    fields = background_trajectories.transpose(1, 0, 2)
    blocks = sensor_spread_matrix.reshape(OWN, HOME, OBS).transpose(1, 0, 2)
    me = lax.axis_index("member").reshape(1)

    to_next, to_prev = pl.pallas_call(
        pick_kernel,
        out_shape=(shape(2 * HANDED, OWN, OBS),) * 2,
        in_specs=[SCALARS, HBM, HBM, HBM],
        out_specs=(WHOLE, WHOLE),
        scratch_shapes=[
            pltpu.VMEM((2 * HANDED, 2, 128), F32),
            pltpu.VMEM((2 * HANDED, 2, 128), F32),
            pltpu.SemaphoreType.DMA((6 * HANDED,)),
        ],
        compiler_params=PARAMS,
        name="pick",
    )(edge_tile_handoff, blocks, val, wgt)
    left = shifted(to_next, 1)
    right = shifted(to_prev, -1)

    about = (me, measurement_tile_table, distance_damping, active_tile_tally, val, wgt)

    def fields_first(fields, blocks, left, right, *about):
        packed = pl.pallas_call(
            pack_both_kernel,
            out_shape=shape(PEERS, LEVELS + 2, OWN, COLS),
            in_specs=[HBM, HBM, ANY, ANY],
            out_specs=ANY,
            scratch_shapes=[pltpu.SemaphoreType.DMA((2 * PEERS,))],
            compiler_params=PARAMS,
            name="pack_both",
        )(fields, blocks, left, right)
        gathered = exchange(packed)
        grams = pl.pallas_call(
            gram_kernel,
            out_shape=shape(PEERS, 2, 8, 256),
            in_specs=[SCALARS] * 4 + [WHOLE] * 5,
            out_specs=WHOLE,
            compiler_params=PARAMS,
            name="gram",
        )(*about, left, right, gathered)
        return finish(exchange(grams), gathered)

    def fields_second(fields, blocks, left, right, *about):
        packed = pl.pallas_call(
            pack_blocks_kernel,
            out_shape=shape(PEERS, 2, OWN, COLS),
            in_specs=[HBM, ANY, ANY],
            out_specs=ANY,
            scratch_shapes=[pltpu.SemaphoreType.DMA((PEERS,))],
            compiler_params=PARAMS,
            name="pack_blocks",
        )(blocks, left, right)
        gathered = exchange(packed)
        grams = pl.pallas_call(
            gram_and_pack_kernel,
            out_shape=shape(PEERS, LEVELS + 2, OWN, COLS),
            in_specs=[SCALARS] * 4 + [WHOLE] * 5 + [HBM],
            out_specs=ANY,
            scratch_shapes=[
                pltpu.VMEM((PEERS, 2, 8, 256), BF16),
                pltpu.SemaphoreType.DMA((PEERS + 1,)),
            ],
            compiler_params=PARAMS,
            name="gram_and_pack",
        )(*about, left, right, gathered, fields)
        entries = exchange(grams)
        return finish(entries, entries)

    operands = (fields, blocks, left, right, *about)
    if SPLIT:
        even = lax.axis_index("region") % 2 == 0
        analysis = lax.cond(even, fields_first, fields_second, *operands)
    else:
        analysis = fields_first(*operands)
    return analysis.transpose(1, 0, 2)


def finish(entries, gathered):
    pert, centre = pl.pallas_call(
        centre_kernel,
        out_shape=(shape(2, MEMBERS, LEVELS * 128), shape(2, 8, LEVELS * 128, dtype=F32)),
        in_specs=[WHOLE],
        out_specs=(WHOLE, WHOLE),
        compiler_params=PARAMS,
        name="centre",
    )(gathered)
    sums = pl.pallas_call(
        combine_kernel,
        out_shape=shape(PEERS, 2, 8, 256),
        in_specs=[WHOLE],
        out_specs=WHOLE,
        compiler_params=PARAMS,
        name="combine",
    )(entries)
    mixed = pl.pallas_call(
        mix_kernel,
        out_shape=shape(PEERS, LEVELS, OWN, COLS),
        in_specs=[WHOLE] * 3,
        out_specs=WHOLE,
        compiler_params=PARAMS,
        name="mix",
    )(exchange(sums), pert, centre)
    return pl.pallas_call(
        unpack_kernel,
        out_shape=shape(LEVELS, OWN, PEERS * COLS),
        in_specs=[ANY],
        out_specs=HBM,
        scratch_shapes=[pltpu.SemaphoreType.DMA((PEERS,))],
        compiler_params=PARAMS,
        name="unpack",
    )(exchange(mixed))


def solution(mesh):
    placed = (
        P("member", None, "region"),
        P("member", "region"),
        P("region"),
        P("region"),
        P(None, "region"),
        P(("region", "member"), None),
        P(("region", "member"), None),
        P(("region", "member")),
    )
    return jax.shard_map(
        on_device,
        mesh=mesh,
        in_specs=placed,
        out_specs=P("member", None, "region"),
        check_vma=False,
    )
```

time: 122 us -> 113 us (0.926)
  blocking collectives: 44.3 us -> 76 us
  waiting for transfers between devices: 41 us -> 13.6 us
  starting transfers between devices: 21.2 us -> 9.82 us
  local copies, waits for them, and re-layouts: 6.18 us -> 2.22 us
  Pallas kernels: 9.08 us -> 10.4 us
    all_to_all x2 -> x3, blocking collectives: 44.3 us -> 76 us  [exchange(): lax.all_to_all(value, 'member', split_axis=0, concat_axis=0, tiled=True)]
    all_to_all x2 -> x1, waiting for transfers between devices: 41 us -> 12 us  [exchange(): lax.all_to_all(value, 'member', split_axis=0, concat_axis=0, tiled=True)]
    all_to_all x2 -> x1, starting transfers between devices: 15.5 us -> 4.26 us  [exchange(): lax.all_to_all(value, 'member', split_axis=0, concat_axis=0, tiled=True)]
    unnamed x21 -> x16, local copies, waits for them, and re-layouts: 4.86 us -> 2.22 us
    ppermute x2, waiting for transfers between devices: 0.01 us -> 1.54 us  [shifted(): return lax.ppermute(value, 'region', pairs)]
    pallas_call x7, Pallas kernels: 9.08 us -> 10.4 us  [the longest x1 2.87 us: finish(): pl.pallas_call(mix_kernel, out_shape=shape(PEERS, LEVELS, OWN, COLS), in_...]
    pallas_call x1 -> x0, local copies, waits for them, and re-layouts: 1.32 us -> none  [on_device(): pl.pallas_call(unpack_kernel, out_shape=shape(OWN, LEVELS, PEERS * COLS),...]
  transfers between devices with their start and end apart: 4 -> 3, of which waited for: 2 -> 2; matrix products, arithmetic and copies ran while one was open for 1% -> 0% of each run, Pallas kernels for 0% -> 0%
where the time goes in v2:
time: 113 us; the launch traced here: 112 us
  blocking collectives  76 us (67%)
  waiting for transfers between devices  13.6 us (12%)
  Pallas kernels  10.4 us (9%)
  starting transfers between devices  9.82 us (9%)
  local copies, waits for them, and re-layouts  2.22 us (2%)
    all_to_all x3, blocking collectives, exchange(): lax.all_to_all(value, 'member', split_axis=0, concat_axis=0, tiled=True)  76 us
    all_to_all x1, waiting for transfers between devices, exchange(): lax.all_to_all(value, 'member', split_axis=0, concat_axis=0, tiled=True)  12 us
    ppermute x2, starting transfers between devices, shifted(): return lax.ppermute(value, 'region', pairs)  5.56 us
    all_to_all x1, starting transfers between devices, exchange(): lax.all_to_all(value, 'member', split_axis=0, concat_axis=0, tiled=True)  4.26 us
    pallas_call x1, Pallas kernels, finish(): pl.pallas_call(mix_kernel, out_shape=shape(PEERS, LEVELS, OWN, COLS), in_...  2.87 us
  transfers between devices with their start and end apart: 3, of which 2 were waited for; matrix products, arithmetic and copies ran while one was open for 0% of the time, Pallas kernels for 0%

profile of v2, /device:TPU:2, one launch (start us, length us, event | category | flops | bytes accessed | tf_op | source)
XLA Modules:
  0.0 112.4 jit_solution(9966485085591397083)
XLA Ops:
  0.0 0.0 copy-start
  0.0 0.0 copy-start.2
  0.0 0.7 copy-done
  0.7 0.0 copy-start.4
  0.7 0.0 copy-start.5
  0.7 1.7 %pick.1 = (bf16[8,8,256]{2,1,0:T(8,128)(2,1)S(1)}, bf16[8,8,256]{2,1,0:T(8,128)(2,1)S(1)}) custom-call(s32[2,4]{1,0:T(2,128)S(1)} %copy-done, bf16[56,8,256]{2,1,0:T(8,128)(2,1)} %bitcast.10, f32[56,2,128]{2,1,0:T(2,128)} %bitcast.13, f32[56,2,128]{2,1,0:T(2,128)} %bitcast.16), custom_call_target="tpu_custom_call" | custom-call | tf_op jit(solution)/shard_map/pick/pallas_call | solution.py:327
  2.4 1.9 %collective-permute-start = (bf16[8,8,256]{2,1,0:T(8,128)(2,1)S(1)}, bf16[8,8,256]{2,1,0:T(8,128)(2,1)S(1)}, u32[]{:S(2)}, u32[]{:S(2)}) collective-permute-start(bf16[8,8,256]{2,1,0:T(8,128)(2,1)S(1)} %get-tuple-element.74), channel_id=1, source_target_pairs={{0,32},{32,64},{64,96},{96,128},{128,160},{160,192},{192,224},{1,3... | collective-permute-start | bytes 98312 | tf_op jit(solution)/shard_map/ppermute | solution.py:300
  4.3 3.6 %collective-permute-start.1 = (bf16[8,8,256]{2,1,0:T(8,128)(2,1)S(1)}, bf16[8,8,256]{2,1,0:T(8,128)(2,1)S(1)}, u32[]{:S(2)}, u32[]{:S(2)}) collective-permute-start(bf16[8,8,256]{2,1,0:T(8,128)(2,1)S(1)} %get-tuple-element.75), channel_id=1, source_target_pairs={{32,0},{64,32},{96,64},{128,96},{160,128},{192,160},{224,192},{33,... | collective-permute-start | bytes 98312 | tf_op jit(solution)/shard_map/ppermute | solution.py:300
  8.0 0.0 copy-start.7
  8.0 0.0 collective-permute-done
  8.0 1.5 %collective-permute-done.1 = bf16[8,8,256]{2,1,0:T(8,128)(2,1)S(1)} collective-permute-done((bf16[8,8,256]{2,1,0:T(8,128)(2,1)S(1)}, bf16[8,8,256]{2,1,0:T(8,128)(2,1)S(1)}, u32[]{:S(2)}, u32[]{:S(2)}) %collective-permute-start.1) | collective-permute-done | bytes 32800 | tf_op jit(solution)/shard_map/ppermute | solution.py:300
  9.5 0.0 copy-start.6
  9.5 0.0 copy-start.8
  9.5 0.0 copy-done.2
  9.5 0.0 copy-done.4
  9.5 0.0 copy-done.5
  9.5 0.0 copy-done.7
  9.6 0.6 copy-done.6
  10.2 0.0 copy-done.8
  10.2 101.3 %conditional.1 = (bf16[6,8,8192]{2,1,0:T(8,128)(2,1)S(1)}) conditional(s32[]{:T(128)} %convert_element_type.3, (bf16[56,8,256]{2,1,0:T(8,128)(2,1)S(1)}, bf16[8,8,256]{2,1,0:T(8,128)(2,1)S(1)}, bf16[8,8,256]{2,1,0:T(8,128)(2,1)S(1)}, s32[1]{0:T(128)}, s32[2,16]{1,0:T(2,128)S(1)}, /*index=5*/f32[2,16]{1,0:T(2,128)S(1)}, s32[2]{0:T(128)S(1)}, ...), branch_computations={%region_0.1_spmd, %region_1.2_spmd} | conditional | bytes 8126532 | solution.py:395
  10.2 1.7 %pack_both.1 = bf16[32,8,8,256]{3,2,1,0:T(8,128)(2,1)S(1)} custom-call(bf16[6,8,8192]{2,1,0:T(8,128)(2,1)} %get-tuple-element.68.fields, bf16[56,8,256]{2,1,0:T(8,128)(2,1)S(1)} %get-tuple-element.69.blocks, bf16[8,8,256]{2,1,0:T(8,128)(2,1)S(1)} %get-tuple-element.66.left, bf16[8,8,256]{2,1,0:T(8,128)(2,1)S(1)} %get-tuple-element.67.right), custom_call_target="tpu_custom_call" | custom-call | tf_op jit(solution)/shard_map/cond/branch_1_fun/pack_both/pallas_call | solution.py:346
  11.9 31.7 %all_to_all.35.gathered.fields = bf16[32,8,8,256]{3,2,1,0:T(8,128)(2,1)S(1)} all-to-all(bf16[32,8,8,256]{3,2,1,0:T(8,128)(2,1)S(1)} %pack_both.1), channel_id=1, replica_groups=mesh['region'=8,'member'=32] {'member'}, dimensions={0} | all-to-all | bytes 2097152 | tf_op jit(solution)/shard_map/cond/branch_1_fun/all_to_all | solution.py:304
  43.7 1.2 %gram.1 = bf16[32,2,8,256]{3,2,1,0:T(8,128)(2,1)S(1)} custom-call(s32[1]{0:T(128)} %get-tuple-element.60.me, s32[2,16]{1,0:T(2,128)S(1)} %get-tuple-element.61.table, f32[2,16]{1,0:T(2,128)S(1)} %get-tuple-element.62.damping, s32[2]{0:T(128)S(1)} %get-tuple-element.63.tally, f32[56,2,128]{2,1,0:T(2,128)S(1)} %get-tuple-element.64.val, ...), custom_call_target="tpu_custom_call" | custom-call | tf_op jit(solution)/shard_map/cond/branch_1_fun/gram/pallas_call | solution.py:356
  44.9 18.8 %all_to_all.36.entries = bf16[32,2,8,256]{3,2,1,0:T(8,128)(2,1)S(1)} all-to-all(bf16[32,2,8,256]{3,2,1,0:T(8,128)(2,1)S(1)} %gram.1), channel_id=1, replica_groups=mesh['region'=8,'member'=32] {'member'}, dimensions={0} | all-to-all | bytes 524288 | tf_op jit(solution)/shard_map/cond/branch_1_fun/all_to_all | solution.py:304
  63.7 2.2 %combine.3 = bf16[32,2,8,256]{3,2,1,0:T(8,128)(2,1)} custom-call(bf16[32,2,8,256]{3,2,1,0:T(8,128)(2,1)S(1)} %all_to_all.36.entries), custom_call_target="tpu_custom_call" | custom-call | tf_op jit(solution)/shard_map/cond/branch_1_fun/combine/pallas_call | solution.py:410
  65.8 4.3 %all-to-all-start.6 = ((bf16[32,2,8,256]{3,2,1,0:T(8,128)(2,1)}), bf16[32,2,8,256]{3,2,1,0:T(8,128)(2,1)S(1)}, u32[]{:S(2)}, u32[]{:S(2)}) async-start(bf16[32,2,8,256]{3,2,1,0:T(8,128)(2,1)} %combine.3), calls=%async_computation.6 | async-start | bytes 524288 | tf_op jit(solution)/shard_map/cond/branch_1_fun/all_to_all | solution.py:304
  70.1 0.3 centre.3
  70.4 12.0 %all-to-all-done.6.entries = bf16[32,2,8,256]{3,2,1,0:T(8,128)(2,1)S(1)} async-done(((bf16[32,2,8,256]{3,2,1,0:T(8,128)(2,1)}), bf16[32,2,8,256]{3,2,1,0:T(8,128)(2,1)S(1)}, u32[]{:S(2)}, u32[]{:S(2)}) %all-to-all-start.6) | async-done | bytes 262176 | tf_op jit(solution)/shard_map/cond/branch_1_fun/all_to_all | solution.py:304
  82.4 2.9 %mix.3 = bf16[32,6,8,256]{3,2,1,0:T(8,128)(2,1)S(1)} custom-call(bf16[32,2,8,256]{3,2,1,0:T(8,128)(2,1)S(1)} %all-to-all-done.6.entries, bf16[2,256,768]{2,1,0:T(8,128)(2,1)S(1)} %get-tuple-element.70.pert, f32[2,8,768]{2,1,0:T(8,128)S(1)} %get-tuple-element.71.centre), custom_call_target="tpu_custom_call" | custom-call | tf_op jit(solution)/shard_map/cond/branch_1_fun/mix/pallas_call | solution.py:418
  85.3 25.5 %all_to_all.37.parts = bf16[32,6,8,256]{3,2,1,0:T(8,128)(2,1)S(1)} all-to-all(bf16[32,6,8,256]{3,2,1,0:T(8,128)(2,1)S(1)} %mix.3), channel_id=1, replica_groups=mesh['region'=8,'member'=32] {'member'}, dimensions={0} | all-to-all | bytes 1572864 | tf_op jit(solution)/shard_map/cond/branch_1_fun/all_to_all | solution.py:304
  110.8 0.5 unpack.3
  111.5 0.0 copy-start.3
  111.5 0.9 copy-done.3
Async XLA Ops:
  0.0 0.7 copy-start
  0.0 9.5 %copy-start.2 = (bf16[8,14336]{1,0:T(8,128)(2,1)S(1)}, bf16[8,14336]{1,0:T(8,128)(2,1)}, u32[]{:S(2)}) copy-start(bf16[8,14336]{1,0:T(8,128)(2,1)} %param.11) | copy-start | bytes 688132
  0.7 8.8 %copy-start.4 = (f32[14336]{0:T(1024)S(1)}, f32[14336]{0:T(1024)}, u32[]{:S(2)}) copy-start(f32[14336]{0:T(1024)} %param.12) | copy-start | bytes 172036
  0.7 8.8 %copy-start.5 = (f32[14336]{0:T(1024)S(1)}, f32[14336]{0:T(1024)}, u32[]{:S(2)}) copy-start(f32[14336]{0:T(1024)} %param.13) | copy-start | bytes 172036
  2.4 5.6 %collective-permute-start = (bf16[8,8,256]{2,1,0:T(8,128)(2,1)S(1)}, bf16[8,8,256]{2,1,0:T(8,128)(2,1)S(1)}, u32[]{:S(2)}, u32[]{:S(2)}) collective-permute-start(bf16[8,8,256]{2,1,0:T(8,128)(2,1)S(1)} %get-tuple-element.74), channel_id=1, source_target_pairs={{0,32},{32,64},{64,96},{96,128},{128,160},{160,192},{192,224},{1,3... | collective-permute-start | bytes 98312 | tf_op jit(solution)/shard_map/ppermute | solution.py:300
  4.3 5.2 %collective-permute-start.1 = (bf16[8,8,256]{2,1,0:T(8,128)(2,1)S(1)}, bf16[8,8,256]{2,1,0:T(8,128)(2,1)S(1)}, u32[]{:S(2)}, u32[]{:S(2)}) collective-permute-start(bf16[8,8,256]{2,1,0:T(8,128)(2,1)S(1)} %get-tuple-element.75), channel_id=1, source_target_pairs={{32,0},{64,32},{96,64},{128,96},{160,128},{192,160},{224,192},{33,... | collective-permute-start | bytes 98312 | tf_op jit(solution)/shard_map/ppermute | solution.py:300
  8.0 1.6 %copy-start.7 = (f32[2,16]{1,0:T(2,128)S(1)}, f32[2,16]{1,0:T(2,128)}, u32[]{:S(2)}) copy-start(f32[2,16]{1,0:T(2,128)} %param.16) | copy-start | bytes 388
  9.5 0.7 copy-start.6
  9.5 0.7 copy-start.8
  65.8 16.6 %all-to-all-start.6 = ((bf16[32,2,8,256]{3,2,1,0:T(8,128)(2,1)}), bf16[32,2,8,256]{3,2,1,0:T(8,128)(2,1)S(1)}, u32[]{:S(2)}, u32[]{:S(2)}) async-start(bf16[32,2,8,256]{3,2,1,0:T(8,128)(2,1)} %combine.3), calls=%async_computation.6 | async-start | bytes 524288 | tf_op jit(solution)/shard_map/cond/branch_1_fun/all_to_all | solution.py:304
  111.5 0.9 copy-start.3

commit v3 on v2

v3 whole, which is shorter than its diff:
```python
import jax
import jax.numpy as jnp
from jax import lax
from jax.experimental import pallas as pl
from jax.experimental.pallas import tpu as pltpu
from jax.sharding import PartitionSpec as P

F32 = jnp.float32
BF16 = jnp.bfloat16
MEMBERS = 256
PEERS = 32
OWN = 8
LEVELS = 6
OBS = 256
HANDED = 4
HOME = 56
EXT = 64
COLS = 256
MAXL = 16
VMEM_BYTES = 48 * 1024 * 1024
WHOLE = pl.BlockSpec(memory_space=pltpu.VMEM)
ANY = pl.BlockSpec(memory_space=pl.ANY)
HBM = pl.BlockSpec(memory_space=pltpu.HBM)
SCALARS = pl.BlockSpec(memory_space=pltpu.SMEM)
PARAMS = pltpu.CompilerParams(vmem_limit_bytes=VMEM_BYTES)


def iota(shape, dim):
    return lax.broadcasted_iota(jnp.int32, shape, dim)


def one_hot_lanes(shape):
    hit = iota(shape, 0) - 64 == (iota(shape, 1) >> 2)
    return jnp.where(hit, 1.0, 0.0).astype(BF16)


def dot(a, b):
    return jnp.dot(a, b, preferred_element_type=F32)


def split(a):
    high = a.astype(BF16)
    return high, (a - high.astype(F32)).astype(BF16)


def product(a, b):
    return dot(a[0], b[0]) + (dot(a[0], b[1]) + dot(a[1], b[0]))


def rounded(a):
    return a.astype(BF16).astype(F32)


def in_flight(pairs, sems):
    copies = [pltpu.make_async_copy(*ends, sems.at[k]) for k, ends in enumerate(pairs)]
    for copy in copies:
        copy.start()
    return copies


def landed(copies):
    for copy in copies:
        copy.wait()


def wide_row(pair):
    return jnp.concatenate([pair[:1], pair[1:]], axis=1)


def own_pairs(blocks, zeros, out, group):
    zeros[...] = jnp.zeros(zeros.shape, BF16)
    return [
        (
            blocks.at[pl.ds(2 * peer, 2)] if 2 * peer < HOME else zeros,
            out.at[peer, pl.ds(group, 2)],
        )
        for peer in range(PEERS)
    ]


def field_pairs(fields, out):
    return [
        (fields.at[:, :, pl.ds(peer * COLS, COLS)], out.at[peer, pl.ds(0, LEVELS)])
        for peer in range(PEERS)
    ]


def pack_both_kernel(fields, blocks, out, zeros, sems):
    pairs = field_pairs(fields, out) + own_pairs(blocks, zeros, out, LEVELS)
    landed(in_flight(pairs, sems))


def pack_blocks_kernel(blocks, out, zeros, sems):
    landed(in_flight(own_pairs(blocks, zeros, out, 0), sems))


def first_half(rows):
    return iota(rows.shape, 1) < 4


def interleaved(first, second):
    first, second = (rows.reshape(16, 8, 256) for rows in (first, second))
    here = first_half(first)
    even = jnp.where(here, first, pltpu.roll(second, 4, 1))
    odd = jnp.where(here, pltpu.roll(first, 4, 1), second)
    return jnp.stack([even, odd], axis=1).reshape(PEERS, 8, 256)


def separated(rows):
    rows = rows.reshape(16, 2, 8, 256)
    even, odd = rows[:, 0], rows[:, 1]
    here = first_half(even)
    first = jnp.where(here, even, pltpu.roll(odd, 4, 1))
    second = jnp.where(here, pltpu.roll(even, 4, 1), odd)
    return first.reshape(128, 256), second.reshape(128, 256)


def grams_of(me, table, damping, tally, val, wgt, pert):
    lane = iota((128, 128), 1)
    row = iota((128, 128), 0) & 3
    slot_of_lane = iota((1, 128), 1) - 64
    top, low = [], []
    for half in range(2):
        own = jnp.minimum(2 * me[0] + half, HOME - 1)
        w, v = wide_row(wgt[own]), wide_row(val[own])
        y = pert(half).astype(F32).reshape(MEMBERS, OBS)
        scaled = (y * w).astype(BF16)
        gram = lax.dot_general(
            y.astype(BF16), scaled, (((1,), (1,)), ((), ())), preferred_element_type=F32
        )
        vector = jnp.sum(y * (w * v), axis=1, keepdims=True)
        vector_high = rounded(vector)
        vector_low = vector - vector_high
        coeff = jnp.zeros((1, 128), F32)
        for position in range(MAXL):
            used = jnp.where(position < tally[half], damping[half, position], 0.0)
            slot = (table[half, position] - HANDED) & (EXT - 1)
            coeff = coeff + jnp.where(slot_of_lane == slot, used, 0.0)
        coeff_high = rounded(coeff)
        extra = jnp.where(row == 0, coeff_high, jnp.where(row == 1, coeff - coeff_high, 0.0))
        for place, column in enumerate(
            (vector_high[:128], vector_low[:128], vector_high[128:], vector_low[128:])
        ):
            extra = jnp.where(lane == place, column, extra)
        top.append(gram[:128, :])
        low.append(jnp.concatenate([gram[128:, 128:], extra], axis=1))
    return interleaved(*top).astype(BF16), interleaved(*low).astype(BF16)


def gram_kernel(me, table, damping, tally, val, wgt, gathered, out):
    out[:, 0], out[:, 1] = grams_of(
        me, table, damping, tally, val, wgt, lambda half: gathered[:, LEVELS + half]
    )


def gram_and_pack_kernel(
    me, table, damping, tally, val, wgt, gathered, fields, out, grams, sems
):
    copies = in_flight(field_pairs(fields, out), sems)
    grams[:, 0], grams[:, 1] = grams_of(
        me, table, damping, tally, val, wgt, lambda half: gathered[:, half]
    )
    last = pltpu.make_async_copy(grams, out.at[:, pl.ds(LEVELS, 2)], sems.at[PEERS])
    last.start()
    landed(copies)
    last.wait()


def choose_kernel(region, chosen, entries, across, within):
    odd = region[0] & 1
    here = iota((2, 8, 256), 1) < 4
    for side, out in ((1 - odd, across), (odd, within)):
        for pair in range(HANDED // 2):
            rows = []
            for k in range(2):
                block = chosen[side, 2 * pair + k]
                x = entries[block >> 1].astype(F32)
                rows.append(jnp.where((block & 1) == k, x, pltpu.roll(x, 4, 1)))
            out[pair] = jnp.where(here, rows[0], rows[1]).astype(BF16)


def combine_kernel(region, entries, across, within, out):
    x = entries[...].astype(F32)
    coeffs = x[:, 1, :, 128:]
    here = first_half(coeffs)
    high = jnp.where(here, coeffs[:, 0:1], coeffs[:, 4:5]).reshape(256, 128)
    low = jnp.where(here, coeffs[:, 1:2], coeffs[:, 5:6]).reshape(256, 128)
    spread_out = one_hot_lanes((128, 256))
    wide = dot(jnp.concatenate([high, low], axis=0).astype(BF16), spread_out)
    same = ((iota((256, 256), 0) ^ iota((256, 256), 1)) & 3) == 0
    high = jnp.where(same, wide[:256], 0.0).astype(BF16)
    low = jnp.where(same, wide[256:], 0.0).astype(BF16)

    odd = (region[0] & 1) == 1
    across, within = across[...].astype(F32), within[...].astype(F32)
    left = jnp.where(odd, within, across)
    right = jnp.where(odd, across, within)
    total = []
    for part in range(2):
        handed = jnp.concatenate([right[:, part], left[:, part]], axis=0)
        if part == 1:
            keep = iota(handed.shape, 2) >= 192
            handed = jnp.where(keep, x[HOME // 2 :, part], handed)
        rows = jnp.concatenate([x[: HOME // 2, part], handed], axis=0)
        rows = rows.reshape(256, 256).astype(BF16)
        total.append(dot(high, rows) + dot(low, rows))
    tail = total[1][:, 128:]
    both = tail + pltpu.roll(tail, 127, 1)
    high = rounded(both)
    low = pltpu.roll(both - high, 1, 1)
    lane = iota((256, 128), 1)
    tail = jnp.where(lane < 4, jnp.where((lane & 1) == 0, high, low), tail)
    tail = jnp.concatenate([total[1][:, :128], tail], axis=1)
    out[:, 0] = total[0].reshape(PEERS, 8, 256).astype(BF16)
    out[:, 1] = tail.reshape(PEERS, 8, 256).astype(BF16)


def centre_kernel(fields, pert, centre, entries=None):
    if entries is not None:
        entries[...] = fields[:, LEVELS:]
    for level in range(LEVELS):
        x = fields[:, level].astype(F32).reshape(MEMBERS, COLS)
        mean = jnp.sum(x, axis=0, keepdims=True) / MEMBERS
        away = (x - mean).astype(BF16)
        for half in range(2):
            at = slice(level * 128, (level + 1) * 128)
            pert[half, :, at] = away[:, half * 128 : (half + 1) * 128]
            centre[half, :, at] = jnp.broadcast_to(
                mean[:, half * 128 : (half + 1) * 128], (8, 128)
            )


def mix_kernel(entries, pert, centre, out):
    x = entries[...].astype(F32)
    tops, lows = separated(x[:, 0]), separated(x[:, 1])
    eye = jnp.where(iota((256, 256), 0) == iota((256, 256), 1), 1.0, 0.0)
    vectors, bounds, a1 = [], [], []
    for half in range(2):
        top, low = tops[half], lows[half]
        gram = jnp.concatenate(
            [top, jnp.concatenate([top[:, 128:].T, low[:, :128]], axis=1)], axis=0
        )
        vectors.append(
            jnp.concatenate(
                [low[:, 128:129] + low[:, 129:130], low[:, 130:131] + low[:, 131:132]], axis=0
            )
        )
        system = eye + gram * (1.0 / (MEMBERS - 1.0))
        sums = jnp.sum(jnp.abs(system), axis=1, keepdims=True)
        bound = jnp.max(sums, axis=0, keepdims=True)
        bounds.append(bound)
        a1.append(system / bound)
    s1 = [split(a) for a in a1]
    a2 = [product(s, s) for s in s1]
    s2 = [split(a) for a in a2]
    a3 = [product(s, t) for s, t in zip(s2, s1)]
    a4 = [product(s, s) for s in s2]
    z2 = [
        2.25 * eye - 2.4375 * a + 1.6875 * b - 0.5625 * c + 0.0625 * d
        for a, b, c, d in zip(a1, a2, a3, a4)
    ]
    t2 = [split(z) for z in z2]
    az = [split(product(s, t)) for s, t in zip(s1, t2)]
    zz = [split(product(t, t)) for t in t2]
    z3 = [1.5 * z - 0.5 * product(a, b) for z, a, b in zip(z2, az, zz)]
    for half in range(2):
        spread = z3[half] / jnp.sqrt(bounds[half])
        inner = jnp.sum(spread * vectors[half], axis=0, keepdims=True)
        shift = jnp.sum(spread * inner, axis=1, keepdims=True) / (MEMBERS - 1.0)
        mixing = (spread + shift).T.astype(BF16)
        result = dot(mixing, pert[half]) + centre[half][:1]
        for level in range(LEVELS):
            rows = result[:, level * 128 : (level + 1) * 128].reshape(PEERS, OWN, 128)
            out[:, level, :, half * 128 : (half + 1) * 128] = rows.astype(BF16)


def unpack_kernel(parts, out, sems):
    copies = [
        pltpu.make_async_copy(
            parts.at[peer], out.at[:, :, pl.ds(peer * COLS, COLS)], sems.at[peer]
        )
        for peer in range(PEERS)
    ]
    for copy in copies:
        copy.start()
    for copy in copies:
        copy.wait()


def swapped(value, first):
    pairs = []
    for i in range(first, lax.axis_size("region") - 1, 2):
        pairs += [(i, i + 1), (i + 1, i)]
    return lax.ppermute(value, "region", pairs)


def exchange(value):
    return lax.all_to_all(value, "member", split_axis=0, concat_axis=0, tiled=True)


def shape(*dims, dtype=BF16):
    return jax.ShapeDtypeStruct(dims, dtype)


CENTRED = (shape(2, MEMBERS, LEVELS * 128), shape(2, 8, LEVELS * 128, dtype=F32))


def on_device(
    background_trajectories,
    sensor_spread_matrix,
    departure_vector,
    inverse_error_variance,
    edge_tile_handoff,
    measurement_tile_table,
    distance_damping,
    active_tile_tally,
):
    val = departure_vector.reshape(HOME, 2, 128)
    wgt = inverse_error_variance.reshape(HOME, 2, 128)
    fields = background_trajectories.transpose(1, 0, 2)
    blocks = sensor_spread_matrix.reshape(OWN, HOME, OBS).transpose(1, 0, 2)
    me = lax.axis_index("member").reshape(1)

    region = lax.axis_index("region").reshape(1)
    about = (me, measurement_tile_table, distance_damping, active_tile_tally, val, wgt)

    def fields_first(fields, blocks, *about):
        packed = pl.pallas_call(
            pack_both_kernel,
            out_shape=shape(PEERS, LEVELS + 2, OWN, COLS),
            in_specs=[HBM, HBM],
            out_specs=ANY,
            scratch_shapes=[
                pltpu.VMEM((2, OWN, COLS), BF16),
                pltpu.SemaphoreType.DMA((2 * PEERS,)),
            ],
            compiler_params=PARAMS,
            name="pack_both",
        )(fields, blocks)
        gathered = exchange(packed)
        grams = pl.pallas_call(
            gram_kernel,
            out_shape=shape(PEERS, 2, 8, 256),
            in_specs=[SCALARS] * 4 + [WHOLE] * 3,
            out_specs=WHOLE,
            compiler_params=PARAMS,
            name="gram",
        )(*about, gathered)
        pert, centre = pl.pallas_call(
            centre_kernel,
            out_shape=CENTRED,
            in_specs=[WHOLE],
            out_specs=(WHOLE,) * 2,
            compiler_params=PARAMS,
            name="centre",
        )(gathered)
        return pert, centre, exchange(grams)

    def fields_second(fields, blocks, *about):
        packed = pl.pallas_call(
            pack_blocks_kernel,
            out_shape=shape(PEERS, 2, OWN, COLS),
            in_specs=[HBM],
            out_specs=ANY,
            scratch_shapes=[
                pltpu.VMEM((2, OWN, COLS), BF16),
                pltpu.SemaphoreType.DMA((PEERS,)),
            ],
            compiler_params=PARAMS,
            name="pack_blocks",
        )(blocks)
        grams = pl.pallas_call(
            gram_and_pack_kernel,
            out_shape=shape(PEERS, LEVELS + 2, OWN, COLS),
            in_specs=[SCALARS] * 4 + [WHOLE] * 3 + [HBM],
            out_specs=ANY,
            scratch_shapes=[
                pltpu.VMEM((PEERS, 2, 8, 256), BF16),
                pltpu.SemaphoreType.DMA((PEERS + 1,)),
            ],
            compiler_params=PARAMS,
            name="gram_and_pack",
        )(*about, exchange(packed), fields)
        return pl.pallas_call(
            centre_kernel,
            out_shape=CENTRED + (shape(PEERS, 2, 8, 256),),
            in_specs=[WHOLE],
            out_specs=(WHOLE,) * 3,
            compiler_params=PARAMS,
            name="centre_and_part",
        )(exchange(grams))

    even = lax.axis_index("region") % 2 == 0
    pert, centre, entries = lax.cond(even, fields_first, fields_second, fields, blocks, *about)

    across, within = pl.pallas_call(
        choose_kernel,
        out_shape=(shape(HANDED // 2, 2, 8, 256),) * 2,
        in_specs=[SCALARS, SCALARS, WHOLE],
        out_specs=(WHOLE, WHOLE),
        compiler_params=PARAMS,
        name="choose",
    )(region, edge_tile_handoff, entries)
    sums = pl.pallas_call(
        combine_kernel,
        out_shape=shape(PEERS, 2, 8, 256),
        in_specs=[SCALARS] + [WHOLE] * 3,
        out_specs=WHOLE,
        compiler_params=PARAMS,
        name="combine",
    )(region, entries, swapped(across, 1), swapped(within, 0))
    mixed = pl.pallas_call(
        mix_kernel,
        out_shape=shape(PEERS, LEVELS, OWN, COLS),
        in_specs=[WHOLE] * 3,
        out_specs=WHOLE,
        compiler_params=PARAMS,
        name="mix",
    )(exchange(sums), pert, centre)
    analysis = pl.pallas_call(
        unpack_kernel,
        out_shape=shape(LEVELS, OWN, PEERS * COLS),
        in_specs=[ANY],
        out_specs=HBM,
        scratch_shapes=[pltpu.SemaphoreType.DMA((PEERS,))],
        compiler_params=PARAMS,
        name="unpack",
    )(exchange(mixed))
    return analysis.transpose(1, 0, 2)


def solution(mesh):
    placed = (
        P("member", None, "region"),
        P("member", "region"),
        P("region"),
        P("region"),
        P(None, "region"),
        P(("region", "member"), None),
        P(("region", "member"), None),
        P(("region", "member")),
    )
    return jax.shard_map(
        on_device,
        mesh=mesh,
        in_specs=placed,
        out_specs=P("member", None, "region"),
        check_vma=False,
    )
```

time: 113 us -> 107 us (0.947)
  blocking collectives: 76 us -> 73.1 us
    all_to_all x3, blocking collectives: 76 us -> 73.1 us  [exchange(): lax.all_to_all(value, 'member', split_axis=0, concat_axis=0, tiled=True)]
    ppermute x2, starting transfers between devices: 5.56 us -> 3.6 us  [swapped(): return lax.ppermute(value, 'region', pairs)]
    all_to_all x1, starting transfers between devices: 4.26 us -> 5.42 us  [exchange(): lax.all_to_all(value, 'member', split_axis=0, concat_axis=0, tiled=True)]
where the time goes in v3:
time: 107 us; the launch traced here: 106 us
  blocking collectives  73.1 us (68%)
  waiting for transfers between devices  12.8 us (12%)
  Pallas kernels  9.8 us (9%)
  starting transfers between devices  9.02 us (8%)
  local copies, waits for them, and re-layouts  1.38 us (1%)
    all_to_all x3, blocking collectives, exchange(): lax.all_to_all(value, 'member', split_axis=0, concat_axis=0, tiled=True)  73.1 us
    all_to_all x1, waiting for transfers between devices, exchange(): lax.all_to_all(value, 'member', split_axis=0, concat_axis=0, tiled=True)  11.3 us
    all_to_all x1, starting transfers between devices, exchange(): lax.all_to_all(value, 'member', split_axis=0, concat_axis=0, tiled=True)  5.42 us
    ppermute x2, starting transfers between devices, swapped(): return lax.ppermute(value, 'region', pairs)  3.6 us
    pallas_call x1, Pallas kernels, on_device(): pl.pallas_call(mix_kernel, out_shape=shape(PEERS, LEVELS, OWN, COLS), in_...  2.55 us
  transfers between devices with their start and end apart: 3, of which 2 were waited for; matrix products, arithmetic and copies ran while one was open for 0% of the time, Pallas kernels for 0%

profile of v3, /device:TPU:2, one launch (start us, length us, event | category | flops | bytes accessed | tf_op | source)
XLA Modules:
  0.0 106.1 jit_solution(8552429839749960933)
XLA Ops:
  0.0 0.0 copy-start.7
  0.0 0.0 copy-start.6
  0.0 0.0 copy-start.8
  0.0 0.7 copy-done.7
  0.7 0.0 copy-done.6
  0.7 0.0 copy-done.8
  0.7 51.1 %conditional.1 = ((bf16[2,256,768]{2,1,0:T(8,128)(2,1)S(1)}, f32[2,8,768]{2,1,0:T(8,128)S(1)}, bf16[32,2,8,256]{3,2,1,0:T(8,128)(2,1)})) conditional(s32[]{:T(128)} %convert_element_type.3, (bf16[56,8,256]{2,1,0:T(8,128)(2,1)}, s32[1]{0:T(128)}, s32[2,16]{1,0:T(2,128)S(1)}, f32[2,16]{1,0:T(2,128)S(1)}, s32[2]{0:T(128)S(1)}, ...), branch_computations={%region_0.1_spmd, %region_1.2_spmd} | conditional | bytes 6226012 | solution.py:394
  0.7 1.8 %pack_both.1 = bf16[32,8,8,256]{3,2,1,0:T(8,128)(2,1)S(1)} custom-call(bf16[6,8,8192]{2,1,0:T(8,128)(2,1)} %get-tuple-element.45.fields, bf16[56,8,256]{2,1,0:T(8,128)(2,1)} %get-tuple-element.46.blocks), custom_call_target="tpu_custom_call" | custom-call | tf_op jit(solution)/shard_map/cond/branch_1_fun/pack_both/pallas_call | solution.py:328
  2.5 0.0 copy-start.3
  2.5 0.0 copy-start.5
  2.5 30.7 %all_to_all.28.fields.gathered = bf16[32,8,8,256]{3,2,1,0:T(8,128)(2,1)S(1)} all-to-all(bf16[32,8,8,256]{3,2,1,0:T(8,128)(2,1)S(1)} %pack_both.1), channel_id=1, replica_groups=mesh['region'=8,'member'=32] {'member'}, dimensions={0} | all-to-all | bytes 2097152 | tf_op jit(solution)/shard_map/cond/branch_1_fun/all_to_all | solution.py:298
  33.2 0.0 copy-done.3
  33.2 0.0 copy-done.5
  33.2 1.6 %gram.1 = bf16[32,2,8,256]{3,2,1,0:T(8,128)(2,1)} custom-call(s32[1]{0:T(128)} %get-tuple-element.49.me, s32[2,16]{1,0:T(2,128)S(1)} %get-tuple-element.50.table, f32[2,16]{1,0:T(2,128)S(1)} %get-tuple-element.51.damping, s32[2]{0:T(128)S(1)} %get-tuple-element.52.tally, f32[56,2,128]{2,1,0:T(2,128)S(1)} %copy-done.3, f32[56,2,128]{2,1,0:T(2,128)S(1)} %copy-done.5, ...), custom_call_target="tpu_custom_call" | custom-call | tf_op jit(solution)/shard_map/cond/branch_1_fun/gram/pallas_call | solution.py:341
  34.8 5.4 %all-to-all-start.3 = ((bf16[32,2,8,256]{3,2,1,0:T(8,128)(2,1)}), bf16[32,2,8,256]{3,2,1,0:T(8,128)(2,1)}, u32[]{:S(2)}, u32[]{:S(2)}) async-start(bf16[32,2,8,256]{3,2,1,0:T(8,128)(2,1)} %gram.1), calls=%async_computation.3 | async-start | bytes 524288 | tf_op jit(solution)/shard_map/cond/branch_1_fun/all_to_all | solution.py:298
  40.2 0.3 centre.1
  40.5 11.3 %all-to-all-done.3 = bf16[32,2,8,256]{3,2,1,0:T(8,128)(2,1)} async-done(((bf16[32,2,8,256]{3,2,1,0:T(8,128)(2,1)}), bf16[32,2,8,256]{3,2,1,0:T(8,128)(2,1)}, u32[]{:S(2)}, u32[]{:S(2)}) %all-to-all-start.3) | async-done | bytes 262176 | tf_op jit(solution)/shard_map/cond/branch_1_fun/all_to_all | solution.py:298
  51.8 0.0 copy-start
  51.8 0.7 copy-done
  52.5 1.0 choose.1
  53.5 1.9 %collective-permute-start = (bf16[2,2,8,256]{3,2,1,0:T(8,128)(2,1)S(1)}, bf16[2,2,8,256]{3,2,1,0:T(8,128)(2,1)S(1)}, u32[]{:S(2)}, u32[]{:S(2)}) collective-permute-start(bf16[2,2,8,256]{3,2,1,0:T(8,128)(2,1)S(1)} %get-tuple-element.61), channel_id=1, source_target_pairs={{32,64},{64,32},{96,128},{128,96},{160,192},{192,160},{33,65},{65,... | collective-permute-start | bytes 49160 | tf_op jit(solution)/shard_map/ppermute | solution.py:294
  55.4 1.7 %collective-permute-start.1 = (bf16[2,2,8,256]{3,2,1,0:T(8,128)(2,1)S(1)}, bf16[2,2,8,256]{3,2,1,0:T(8,128)(2,1)S(1)}, u32[]{:S(2)}, u32[]{:S(2)}) collective-permute-start(bf16[2,2,8,256]{3,2,1,0:T(8,128)(2,1)S(1)} %get-tuple-element.62), channel_id=1, source_target_pairs={{0,32},{32,0},{64,96},{96,64},{128,160},{160,128},{192,224},{224,1... | collective-permute-start | bytes 49160 | tf_op jit(solution)/shard_map/ppermute | solution.py:294
  57.1 1.4 %collective-permute-done.across = bf16[2,2,8,256]{3,2,1,0:T(8,128)(2,1)S(1)} collective-permute-done((bf16[2,2,8,256]{3,2,1,0:T(8,128)(2,1)S(1)}, bf16[2,2,8,256]{3,2,1,0:T(8,128)(2,1)S(1)}, u32[]{:S(2)}, u32[]{:S(2)}) %collective-permute-start) | collective-permute-done | bytes 16416 | tf_op jit(solution)/shard_map/ppermute | solution.py:294
  58.5 0.0 collective-permute-done.1.within
  58.5 1.5 %combine.1 = bf16[32,2,8,256]{3,2,1,0:T(8,128)(2,1)S(1)} custom-call(s32[1]{0:T(128)} %bitcast.region, bf16[32,2,8,256]{3,2,1,0:T(8,128)(2,1)} %get-tuple-element.60.entries, bf16[2,2,8,256]{3,2,1,0:T(8,128)(2,1)S(1)} %collective-permute-done.across, bf16[2,2,8,256]{3,2,1,0:T(8,128)(2,1)S(1)} %collective-permute-done.1.within), custom_call_target="tpu_custom_call" | custom-call | tf_op jit(solution)/shard_map/combine/pallas_call | solution.py:404
  60.0 16.8 %all_to_all.29.entries = bf16[32,2,8,256]{3,2,1,0:T(8,128)(2,1)S(1)} all-to-all(bf16[32,2,8,256]{3,2,1,0:T(8,128)(2,1)S(1)} %combine.1), channel_id=1, replica_groups=mesh['region'=8,'member'=32] {'member'}, dimensions={0} | all-to-all | bytes 524288 | tf_op jit(solution)/shard_map/all_to_all | solution.py:298
  76.8 2.5 %mix.1 = bf16[32,6,8,256]{3,2,1,0:T(8,128)(2,1)S(1)} custom-call(bf16[32,2,8,256]{3,2,1,0:T(8,128)(2,1)S(1)} %all_to_all.29.entries, bf16[2,256,768]{2,1,0:T(8,128)(2,1)S(1)} %get-tuple-element.63.pert, f32[2,8,768]{2,1,0:T(8,128)S(1)} %get-tuple-element.64.centre), custom_call_target="tpu_custom_call" | custom-call | tf_op jit(solution)/shard_map/mix/pallas_call | solution.py:412
  79.4 25.6 %all_to_all.30.parts = bf16[32,6,8,256]{3,2,1,0:T(8,128)(2,1)S(1)} all-to-all(bf16[32,6,8,256]{3,2,1,0:T(8,128)(2,1)S(1)} %mix.1), channel_id=1, replica_groups=mesh['region'=8,'member'=32] {'member'}, dimensions={0} | all-to-all | bytes 1572864 | tf_op jit(solution)/shard_map/all_to_all | solution.py:298
  105.0 1.1 %unpack.1 = bf16[6,8,8192]{2,1,0:T(8,128)(2,1)} custom-call(bf16[32,6,8,256]{3,2,1,0:T(8,128)(2,1)S(1)} %all_to_all.30.parts), custom_call_target="tpu_custom_call" | custom-call | tf_op jit(solution)/shard_map/unpack/pallas_call | solution.py:420
Async XLA Ops:
  0.0 0.7 copy-start.7
  0.0 0.7 copy-start.6
  0.0 0.7 copy-start.8
  2.5 30.7 %copy-start.3 = (f32[56,2,128]{2,1,0:T(2,128)S(1)}, f32[56,2,128]{2,1,0:T(2,128)}, u32[]{:S(2)}) copy-start(f32[56,2,128]{2,1,0:T(2,128)} %get-tuple-element.53.val) | copy-start | bytes 172036 | tf_op jit(solution)/shard_map/cond
  2.5 30.7 %copy-start.5 = (f32[56,2,128]{2,1,0:T(2,128)S(1)}, f32[56,2,128]{2,1,0:T(2,128)}, u32[]{:S(2)}) copy-start(f32[56,2,128]{2,1,0:T(2,128)} %get-tuple-element.54.wgt) | copy-start | bytes 172036 | tf_op jit(solution)/shard_map/cond
  34.8 17.0 %all-to-all-start.3 = ((bf16[32,2,8,256]{3,2,1,0:T(8,128)(2,1)}), bf16[32,2,8,256]{3,2,1,0:T(8,128)(2,1)}, u32[]{:S(2)}, u32[]{:S(2)}) async-start(bf16[32,2,8,256]{3,2,1,0:T(8,128)(2,1)} %gram.1), calls=%async_computation.3 | async-start | bytes 524288 | tf_op jit(solution)/shard_map/cond/branch_1_fun/all_to_all | solution.py:298
  51.8 0.7 copy-start
  53.5 5.1 %collective-permute-start = (bf16[2,2,8,256]{3,2,1,0:T(8,128)(2,1)S(1)}, bf16[2,2,8,256]{3,2,1,0:T(8,128)(2,1)S(1)}, u32[]{:S(2)}, u32[]{:S(2)}) collective-permute-start(bf16[2,2,8,256]{3,2,1,0:T(8,128)(2,1)S(1)} %get-tuple-element.61), channel_id=1, source_target_pairs={{32,64},{64,32},{96,128},{128,96},{160,192},{192,160},{33,65},{65,... | collective-permute-start | bytes 49160 | tf_op jit(solution)/shard_map/ppermute | solution.py:294
  55.4 3.1 %collective-permute-start.1 = (bf16[2,2,8,256]{3,2,1,0:T(8,128)(2,1)S(1)}, bf16[2,2,8,256]{3,2,1,0:T(8,128)(2,1)S(1)}, u32[]{:S(2)}, u32[]{:S(2)}) collective-permute-start(bf16[2,2,8,256]{3,2,1,0:T(8,128)(2,1)S(1)} %get-tuple-element.62), channel_id=1, source_target_pairs={{0,32},{32,0},{64,96},{96,64},{128,160},{160,128},{192,224},{224,1... | collective-permute-start | bytes 49160 | tf_op jit(solution)/shard_map/ppermute | solution.py:294

commit v4 on v3

v4 whole, which is shorter than its diff:
```python
import jax
import jax.numpy as jnp
from jax import lax
from jax.experimental import pallas as pl
from jax.experimental.pallas import tpu as pltpu
from jax.sharding import PartitionSpec as P

F32 = jnp.float32
BF16 = jnp.bfloat16
MEMBERS = 256
PEERS = 32
OWN = 8
LEVELS = 6
OBS = 256
HANDED = 4
HOME = 56
EXT = 64
COLS = 256
MAXL = 16
VMEM_BYTES = 48 * 1024 * 1024
WHOLE = pl.BlockSpec(memory_space=pltpu.VMEM)
ANY = pl.BlockSpec(memory_space=pl.ANY)
HBM = pl.BlockSpec(memory_space=pltpu.HBM)
SCALARS = pl.BlockSpec(memory_space=pltpu.SMEM)
PARAMS = pltpu.CompilerParams(vmem_limit_bytes=VMEM_BYTES)


def iota(shape, dim):
    return lax.broadcasted_iota(jnp.int32, shape, dim)


def one_hot_lanes(shape):
    hit = iota(shape, 0) - 64 == (iota(shape, 1) >> 2)
    return jnp.where(hit, 1.0, 0.0).astype(BF16)


def dot(a, b):
    return jnp.dot(a, b, preferred_element_type=F32)


def split(a):
    high = a.astype(BF16)
    return high, (a - high.astype(F32)).astype(BF16)


def product(a, b):
    return dot(a[0], b[0]) + (dot(a[0], b[1]) + dot(a[1], b[0]))


def rounded(a):
    return a.astype(BF16).astype(F32)


def in_flight(pairs, sems):
    copies = [pltpu.make_async_copy(*ends, sems.at[k]) for k, ends in enumerate(pairs)]
    for copy in copies:
        copy.start()
    return copies


def landed(copies):
    for copy in copies:
        copy.wait()


def wide_row(pair):
    return jnp.concatenate([pair[:1], pair[1:]], axis=1)


def block_pairs(region, blocks, across, within, slots, out, group):
    odd = (region[0] & 1) == 1
    across = across[:HANDED].astype(F32)
    within = within[:HANDED].astype(F32)
    right = jnp.where(odd, across, within).astype(BF16)
    left = jnp.where(odd, within, across).astype(BF16)
    slots[: HANDED // 2] = right.reshape(HANDED // 2, 2, OWN, OBS)
    slots[HANDED // 2 :] = left.reshape(HANDED // 2, 2, OWN, OBS)
    return [
        (blocks, out.at[pl.ds(0, HOME // 2), pl.ds(group, 2)]),
        (slots, out.at[pl.ds(HOME // 2, HANDED), pl.ds(group, 2)]),
    ]


def field_pairs(fields, out):
    return [(fields.at[level], out.at[:, level]) for level in range(LEVELS)]


def pack_both_kernel(region, fields, blocks, across, within, out, slots, sems, field_sems):
    first = in_flight(field_pairs(fields, out), field_sems)
    pairs = block_pairs(region, blocks, across, within, slots, out, LEVELS)
    landed(first + in_flight(pairs, sems))


def pack_blocks_kernel(region, blocks, across, within, out, slots, sems):
    pairs = block_pairs(region, blocks, across, within, slots, out, 0)
    landed(in_flight(pairs, sems))


def first_half(rows):
    return iota(rows.shape, 1) < 4


def interleaved(first, second):
    first, second = (rows.reshape(16, 8, 256) for rows in (first, second))
    here = first_half(first)
    even = jnp.where(here, first, pltpu.roll(second, 4, 1))
    odd = jnp.where(here, pltpu.roll(first, 4, 1), second)
    return jnp.stack([even, odd], axis=1).reshape(PEERS, 8, 256)


def separated(rows):
    rows = rows.reshape(16, 2, 8, 256)
    even, odd = rows[:, 0], rows[:, 1]
    here = first_half(even)
    first = jnp.where(here, even, pltpu.roll(odd, 4, 1))
    second = jnp.where(here, pltpu.roll(even, 4, 1), odd)
    return first.reshape(128, 256), second.reshape(128, 256)


def grams_of(me, region, lists, val, wgt, across, within, gathered, group):
    lane = iota((128, 128), 1)
    row = iota((128, 128), 0) & 3
    top, low = [], []
    for half in range(2):
        slot = 2 * me[0] + half
        own = jnp.minimum(slot, HOME - 1)
        slot = jnp.maximum(slot - HOME, 0)
        from_right = jnp.where(slot < HANDED, 1, 0)
        place = HANDED + (slot & (HANDED - 1))
        handed = jnp.where(
            (region[0] & 1) == from_right,
            across[place].astype(F32),
            within[place].astype(F32),
        )
        is_own = 2 * me[0] + half < HOME
        w = jnp.where(is_own, wide_row(wgt[own]), handed[0:1] + handed[1:2])
        v = jnp.where(is_own, wide_row(val[own]), handed[2:3] + handed[3:4])
        y = gathered[:, group + half].astype(F32).reshape(MEMBERS, OBS)
        scaled = (y * w).astype(BF16)
        gram = lax.dot_general(
            y.astype(BF16), scaled, (((1,), (1,)), ((), ())), preferred_element_type=F32
        )
        vector = jnp.sum(y * (w * v), axis=1, keepdims=True)
        vector_high = rounded(vector)
        vector_low = vector - vector_high
        coeff = lists[8 * half : 8 * half + 1]
        coeff_high = rounded(coeff)
        extra = jnp.where(row == 0, coeff_high, jnp.where(row == 1, coeff - coeff_high, 0.0))
        for place, column in enumerate(
            (vector_high[:128], vector_low[:128], vector_high[128:], vector_low[128:])
        ):
            extra = jnp.where(lane == place, column, extra)
        top.append(gram[:128, :])
        low.append(jnp.concatenate([gram[128:, 128:], extra], axis=1))
    return interleaved(*top).astype(BF16), interleaved(*low).astype(BF16)


def gram_kernel(*refs):
    *about, gathered, out = refs
    out[:, 0], out[:, 1] = grams_of(*about, gathered, gathered.shape[1] - 2)


def pick_kernel(region, chosen, blocks, val, wgt, across, within, vals, wgts, sems):
    odd = region[0] & 1
    sides = ((1 - odd, across), (odd, within))
    pairs = [(val, vals), (wgt, wgts)]
    for side, out in sides:
        for k in range(HANDED):
            pairs.append((blocks.at[chosen[side, k]], out.at[k]))
    landed(in_flight(pairs, sems))
    row = iota((OWN, OBS), 0)
    for side, out in sides:
        for k in range(HANDED):
            block = chosen[side, k]
            w, v = wide_row(wgts[block]), wide_row(vals[block])
            w_high, v_high = rounded(w), rounded(v)
            tail = jnp.where(row == 2, v_high, jnp.where(row == 3, v - v_high, 0.0))
            tail = jnp.where(row == 0, w_high, jnp.where(row == 1, w - w_high, tail))
            out[HANDED + k] = tail.astype(BF16)


def lists_kernel(table, damping, tally, out):
    slot_of_lane = iota((1, 128), 1) - 64
    for half in range(2):
        coeff = jnp.zeros((1, 128), F32)
        for position in range(MAXL):
            used = jnp.where(position < tally[half], damping[half, position], 0.0)
            slot = (table[half, position] - HANDED) & (EXT - 1)
            coeff = coeff + jnp.where(slot_of_lane == slot, used, 0.0)
        out[half * 8 : (half + 1) * 8] = jnp.broadcast_to(coeff, (8, 128))


def sums_of(x):
    coeffs = x[:, 1, :, 128:]
    here = first_half(coeffs)
    high = jnp.where(here, coeffs[:, 0:1], coeffs[:, 4:5]).reshape(256, 128)
    low = jnp.where(here, coeffs[:, 1:2], coeffs[:, 5:6]).reshape(256, 128)
    spread_out = one_hot_lanes((128, 256))
    wide = dot(jnp.concatenate([high, low], axis=0).astype(BF16), spread_out)
    same = ((iota((256, 256), 0) ^ iota((256, 256), 1)) & 3) == 0
    high = jnp.where(same, wide[:256], 0.0).astype(BF16)
    low = jnp.where(same, wide[256:], 0.0).astype(BF16)
    total = []
    for part in range(2):
        rows = x[:, part].reshape(256, 256).astype(BF16)
        total.append(dot(high, rows) + dot(low, rows))
    tail = total[1][:, 128:]
    both = tail + pltpu.roll(tail, 127, 1)
    high = rounded(both)
    low = pltpu.roll(both - high, 1, 1)
    lane = iota((256, 128), 1)
    tail = jnp.where(lane < 4, jnp.where((lane & 1) == 0, high, low), tail)
    tail = jnp.concatenate([total[1][:, :128], tail], axis=1)
    return (rows.reshape(PEERS, 8, 256).astype(BF16) for rows in (total[0], tail))


def combine_kernel(entries, fields, out, pert, centre):
    centre_kernel(fields, pert, centre)
    out[:, 0], out[:, 1] = sums_of(entries[...].astype(F32))


def combine_and_pack_kernel(entries, fields, out, part, sems):
    copies = in_flight(field_pairs(fields, out), sems)
    part[:, 0], part[:, 1] = sums_of(entries[...].astype(F32))
    last = pltpu.make_async_copy(part, out.at[:, pl.ds(LEVELS, 2)], sems.at[LEVELS])
    last.start()
    landed(copies)
    last.wait()


def centre_kernel(fields, pert, centre, entries=None):
    if entries is not None:
        entries[...] = fields[:, LEVELS:]
    for level in range(LEVELS):
        x = fields[:, level].astype(F32).reshape(MEMBERS, COLS)
        mean = jnp.sum(x, axis=0, keepdims=True) / MEMBERS
        away = (x - mean).astype(BF16)
        for half in range(2):
            at = slice(level * 128, (level + 1) * 128)
            pert[half, :, at] = away[:, half * 128 : (half + 1) * 128]
            centre[half, :, at] = jnp.broadcast_to(
                mean[:, half * 128 : (half + 1) * 128], (8, 128)
            )


def mix_kernel(entries, pert, centre, out):
    x = entries[...].astype(F32)
    tops, lows = separated(x[:, 0]), separated(x[:, 1])
    eye = jnp.where(iota((256, 256), 0) == iota((256, 256), 1), 1.0, 0.0)
    vectors, bounds, a1 = [], [], []
    for half in range(2):
        top, low = tops[half], lows[half]
        gram = jnp.concatenate(
            [top, jnp.concatenate([top[:, 128:].T, low[:, :128]], axis=1)], axis=0
        )
        vectors.append(
            jnp.concatenate(
                [low[:, 128:129] + low[:, 129:130], low[:, 130:131] + low[:, 131:132]], axis=0
            )
        )
        system = eye + gram * (1.0 / (MEMBERS - 1.0))
        sums = jnp.sum(jnp.abs(system), axis=1, keepdims=True)
        bound = jnp.max(sums, axis=0, keepdims=True)
        bounds.append(bound)
        a1.append(system / bound)
    s1 = [split(a) for a in a1]
    a2 = [product(s, s) for s in s1]
    s2 = [split(a) for a in a2]
    a3 = [product(s, t) for s, t in zip(s2, s1)]
    a4 = [product(s, s) for s in s2]
    z2 = [
        2.25 * eye - 2.4375 * a + 1.6875 * b - 0.5625 * c + 0.0625 * d
        for a, b, c, d in zip(a1, a2, a3, a4)
    ]
    t2 = [split(z) for z in z2]
    az = [split(product(s, t)) for s, t in zip(s1, t2)]
    zz = [split(product(t, t)) for t in t2]
    z3 = [1.5 * z - 0.5 * product(a, b) for z, a, b in zip(z2, az, zz)]
    for half in range(2):
        spread = z3[half] / jnp.sqrt(bounds[half])
        inner = jnp.sum(spread * vectors[half], axis=0, keepdims=True)
        shift = jnp.sum(spread * inner, axis=1, keepdims=True) / (MEMBERS - 1.0)
        mixing = (spread + shift).T.astype(BF16)
        result = dot(mixing, pert[half]) + centre[half][:1]
        for level in range(LEVELS):
            rows = result[:, level * 128 : (level + 1) * 128].reshape(PEERS, OWN, 128)
            out[:, level, :, half * 128 : (half + 1) * 128] = rows.astype(BF16)


def unpack_kernel(parts, out, sems):
    landed(in_flight([(parts.at[:, level], out.at[level]) for level in range(LEVELS)], sems))


def swapped(value, first):
    pairs = []
    for i in range(first, lax.axis_size("region") - 1, 2):
        pairs += [(i, i + 1), (i + 1, i)]
    return lax.ppermute(value, "region", pairs)


def exchange(value):
    return lax.all_to_all(value, "member", split_axis=0, concat_axis=0, tiled=True)


def shape(*dims, dtype=BF16):
    return jax.ShapeDtypeStruct(dims, dtype)


CENTRED = (shape(2, MEMBERS, LEVELS * 128), shape(2, 8, LEVELS * 128, dtype=F32))


WITH_FIELDS = [pltpu.VMEM((PEERS, 2, 8, 256), BF16), pltpu.SemaphoreType.DMA((LEVELS + 1,))]


def on_device(
    background_trajectories,
    sensor_spread_matrix,
    departure_vector,
    inverse_error_variance,
    edge_tile_handoff,
    measurement_tile_table,
    distance_damping,
    active_tile_tally,
):
    val = departure_vector.reshape(HOME, 2, 128)
    wgt = inverse_error_variance.reshape(HOME, 2, 128)
    fields = background_trajectories.reshape(OWN, LEVELS, PEERS, COLS).transpose(1, 2, 0, 3)
    blocks = sensor_spread_matrix.reshape(OWN, HOME, OBS).transpose(1, 0, 2)
    me = lax.axis_index("member").reshape(1)

    region = lax.axis_index("region").reshape(1)
    lists = pl.pallas_call(
        lists_kernel,
        out_shape=shape(16, 128, dtype=F32),
        in_specs=[SCALARS] * 3,
        out_specs=WHOLE,
        compiler_params=PARAMS,
        name="lists",
    )(measurement_tile_table, distance_damping, active_tile_tally)

    across, within = pl.pallas_call(
        pick_kernel,
        out_shape=(shape(2 * HANDED, OWN, OBS),) * 2,
        in_specs=[SCALARS, SCALARS, HBM, HBM, HBM],
        out_specs=(WHOLE, WHOLE),
        scratch_shapes=[
            pltpu.VMEM((HOME, 2, 128), F32),
            pltpu.VMEM((HOME, 2, 128), F32),
            pltpu.SemaphoreType.DMA((2 * HANDED + 2,)),
        ],
        compiler_params=PARAMS,
        name="pick",
    )(region, edge_tile_handoff, blocks, val, wgt)
    across = swapped(across, 1)
    within = swapped(within, 0)

    def gram(gathered, *about):
        return pl.pallas_call(
            gram_kernel,
            out_shape=shape(PEERS, 2, 8, 256),
            in_specs=[SCALARS] * 2 + [WHOLE] * 6,
            out_specs=WHOLE,
            compiler_params=PARAMS,
            name="gram",
        )(*about, gathered)

    def fields_first(fields, blocks, *about):
        _, region, *_, across, within = about
        packed = pl.pallas_call(
            pack_both_kernel,
            out_shape=shape(PEERS, LEVELS + 2, OWN, COLS),
            in_specs=[SCALARS, HBM, HBM, WHOLE, WHOLE],
            out_specs=ANY,
            scratch_shapes=[
                pltpu.VMEM((HANDED, 2, OWN, COLS), BF16),
                pltpu.SemaphoreType.DMA((2,)),
                pltpu.SemaphoreType.DMA((LEVELS,)),
            ],
            compiler_params=PARAMS,
            name="pack_both",
        )(region, fields, blocks, across, within)
        gathered = exchange(packed)
        grams = exchange(gram(gathered, *about))
        sums, pert, centre = pl.pallas_call(
            combine_kernel,
            out_shape=(shape(PEERS, 2, 8, 256),) + CENTRED,
            in_specs=[WHOLE] * 2,
            out_specs=(WHOLE,) * 3,
            compiler_params=PARAMS,
            name="combine",
        )(grams, gathered)
        return pert, centre, exchange(sums)

    def fields_last(fields, blocks, *about):
        _, region, *_, across, within = about
        packed = pl.pallas_call(
            pack_blocks_kernel,
            out_shape=shape(PEERS, 2, OWN, COLS),
            in_specs=[SCALARS, HBM, WHOLE, WHOLE],
            out_specs=ANY,
            scratch_shapes=[
                pltpu.VMEM((HANDED, 2, OWN, COLS), BF16),
                pltpu.SemaphoreType.DMA((2,)),
            ],
            compiler_params=PARAMS,
            name="pack_blocks",
        )(region, blocks, across, within)
        grams = exchange(gram(exchange(packed), *about))
        sums = pl.pallas_call(
            combine_and_pack_kernel,
            out_shape=shape(PEERS, LEVELS + 2, OWN, COLS),
            in_specs=[WHOLE, HBM],
            out_specs=ANY,
            scratch_shapes=WITH_FIELDS,
            compiler_params=PARAMS,
            name="combine_and_pack",
        )(grams, fields)
        return pl.pallas_call(
            centre_kernel,
            out_shape=CENTRED + (shape(PEERS, 2, 8, 256),),
            in_specs=[WHOLE],
            out_specs=(WHOLE,) * 3,
            compiler_params=PARAMS,
            name="centre_and_part",
        )(exchange(sums))

    even = lax.axis_index("region") % 2 == 0
    about = (me, region, lists, val, wgt, across, within)
    pert, centre, systems = lax.cond(
        even,
        fields_first,
        fields_last,
        fields,
        blocks.reshape(HOME // 2, 2, OWN, OBS),
        *about,
    )

    mixed = pl.pallas_call(
        mix_kernel,
        out_shape=shape(PEERS, LEVELS, OWN, COLS),
        in_specs=[WHOLE] * 3,
        out_specs=WHOLE,
        compiler_params=PARAMS,
        name="mix",
    )(systems, pert, centre)
    analysis = pl.pallas_call(
        unpack_kernel,
        out_shape=shape(LEVELS, PEERS, OWN, COLS),
        in_specs=[ANY],
        out_specs=HBM,
        scratch_shapes=[pltpu.SemaphoreType.DMA((LEVELS,))],
        compiler_params=PARAMS,
        name="unpack",
    )(exchange(mixed))
    return analysis.transpose(2, 0, 1, 3).reshape(OWN, LEVELS, PEERS * COLS)


def solution(mesh):
    placed = (
        P("member", None, "region"),
        P("member", "region"),
        P("region"),
        P("region"),
        P(None, "region"),
        P(("region", "member"), None),
        P(("region", "member"), None),
        P(("region", "member")),
    )
    return jax.shard_map(
        on_device,
        mesh=mesh,
        in_specs=placed,
        out_specs=P("member", None, "region"),
        check_vma=False,
    )
```

time: 107 us -> 98.7 us (0.922)
  waiting for transfers between devices: 12.8 us -> 0.3 us
  blocking collectives: 73.1 us -> 84.9 us
  starting transfers between devices: 9.02 us -> 3.6 us
  Pallas kernels: 9.8 us -> 8.05 us
    all_to_all x3 -> x4, blocking collectives: 73.1 us -> 84.9 us  [exchange(): lax.all_to_all(value, 'member', split_axis=0, concat_axis=0, tiled=True)]
    all_to_all x1 -> x0, waiting for transfers between devices: 11.3 us -> none  [exchange(): lax.all_to_all(value, 'member', split_axis=0, concat_axis=0, tiled=True)]
    all_to_all x1 -> x0, starting transfers between devices: 5.42 us -> none  [exchange(): lax.all_to_all(value, 'member', split_axis=0, concat_axis=0, tiled=True)]
    pallas_call x5, Pallas kernels: 5.49 us -> 4.22 us  [the longest x1 1.54 us: on_device(): pl.pallas_call(pick_kernel, out_shape=(shape(2 * HANDED, OWN, OBS),) * 2,...]
    ppermute x2, waiting for transfers between devices: 1.45 us -> 0.3 us  [swapped(): return lax.ppermute(value, 'region', pairs)]
  transfers between devices with their start and end apart: 3 -> 2, of which waited for: 2 -> 1; matrix products, arithmetic and copies ran while one was open for 0% -> 0% of each run, Pallas kernels for 0% -> 1%
where the time goes in v4:
time: 98.7 us; the launch traced here: 98.3 us
  blocking collectives  84.9 us (86%)
  Pallas kernels  8.05 us (8%)
  starting transfers between devices  3.6 us (4%)
  local copies, waits for them, and re-layouts  1.38 us (1%)
    all_to_all x4, blocking collectives, exchange(): lax.all_to_all(value, 'member', split_axis=0, concat_axis=0, tiled=True)  84.9 us
    ppermute x2, starting transfers between devices, swapped(): return lax.ppermute(value, 'region', pairs)  3.6 us
    pallas_call x1, Pallas kernels, on_device(): pl.pallas_call(mix_kernel, out_shape=shape(PEERS, LEVELS, OWN, COLS), in_...  2.55 us
  transfers between devices with their start and end apart: 2, of which 1 were waited for; matrix products, arithmetic and copies ran while one was open for 0% of the time, Pallas kernels for 1%

profile of v4, /device:TPU:2, one launch (start us, length us, event | category | flops | bytes accessed | tf_op | source)
XLA Modules:
  0.0 98.3 jit_solution(806739529536984631)
XLA Ops:
  0.0 0.0 copy-start
  0.0 0.0 copy-start.5
  0.0 0.7 copy-done
  0.7 0.0 copy-start.6
  0.7 0.0 copy-start.7
  0.7 1.5 %pick.1 = (bf16[8,8,256]{2,1,0:T(8,128)(2,1)S(1)}, bf16[8,8,256]{2,1,0:T(8,128)(2,1)S(1)}) custom-call(s32[1]{0:T(128)} %bitcast.region, s32[2,4]{1,0:T(2,128)S(1)} %copy-done, bf16[56,8,256]{2,1,0:T(8,128)(2,1)} %bitcast.17, f32[56,2,128]{2,1,0:T(2,128)} %bitcast.20, f32[56,2,128]{2,1,0:T(2,128)} %bitcast.23), custom_call_target="tpu_custom_call" | custom-call | tf_op jit(solution)/shard_map/pick/pallas_call | solution.py:341
  2.2 1.9 %collective-permute-start = (bf16[8,8,256]{2,1,0:T(8,128)(2,1)S(1)}, bf16[8,8,256]{2,1,0:T(8,128)(2,1)S(1)}, u32[]{:S(2)}, u32[]{:S(2)}) collective-permute-start(bf16[8,8,256]{2,1,0:T(8,128)(2,1)S(1)} %get-tuple-element.67), channel_id=1, source_target_pairs={{32,64},{64,32},{96,128},{128,96},{160,192},{192,160},{33,65},{65,... | collective-permute-start | bytes 98312 | tf_op jit(solution)/shard_map/ppermute | solution.py:298
  4.2 1.7 %collective-permute-start.1 = (bf16[8,8,256]{2,1,0:T(8,128)(2,1)S(1)}, bf16[8,8,256]{2,1,0:T(8,128)(2,1)S(1)}, u32[]{:S(2)}, u32[]{:S(2)}) collective-permute-start(bf16[8,8,256]{2,1,0:T(8,128)(2,1)S(1)} %get-tuple-element.68), channel_id=1, source_target_pairs={{0,32},{32,0},{64,96},{96,64},{128,160},{160,128},{192,224},{224,1... | collective-permute-start | bytes 98312 | tf_op jit(solution)/shard_map/ppermute | solution.py:298
  5.8 0.0 copy-start.2
  5.8 0.0 copy-start.1
  5.8 0.0 copy-start.3
  5.8 0.7 copy-done.2
  6.5 0.0 copy-done.1
  6.5 0.0 copy-done.3
  6.5 0.6 lists.1
  7.2 0.3 collective-permute-done
  7.5 0.0 collective-permute-done.1
  7.5 0.0 copy-done.5
  7.5 0.0 copy-done.6
  7.5 0.0 copy-done.7
  7.5 65.1 %conditional.1 = ((bf16[2,256,768]{2,1,0:T(8,128)(2,1)S(1)}, f32[2,8,768]{2,1,0:T(8,128)S(1)}, bf16[32,2,8,256]{3,2,1,0:T(8,128)(2,1)S(1)})) conditional(s32[]{:T(128)} %convert_element_type.3, (s32[1]{0:T(128)}, bf16[28,2,8,256]{3,2,1,0:T(8,128)(2,1)S(1)}, bf16[8,8,256]{2,1,0:T(8,128)(2,1)S(1)}, bf16[8,8,256]{2,1,0:T(8,128)(2,1)S(1)}, s32[1]{0:T(128)}, ...), branch_computations={%region_0.1_spmd, %region_1.2_spmd} | conditional | bytes 6291492 | solution.py:429
  7.5 1.3 %pack_both.1 = bf16[32,8,8,256]{3,2,1,0:T(8,128)(2,1)S(1)} custom-call(s32[1]{0:T(128)} %get-tuple-element.51.region.refs_1_, bf16[6,32,8,256]{3,2,1,0:T(8,128)(2,1)} %get-tuple-element.57.fields, bf16[28,2,8,256]{3,2,1,0:T(8,128)(2,1)S(1)} %get-tuple-element.58.blocks, bf16[8,8,256]{2,1,0:T(8,128)(2,1)S(1)} %get-tuple-element.55.across.refs_5_, ...), custom_call_target="tpu_custom_call" | custom-call | tf_op jit(solution)/shard_map/cond/branch_1_fun/pack_both/pallas_call | solution.py:369
  8.8 30.6 %all_to_all.32.refs_7_.fields = bf16[32,8,8,256]{3,2,1,0:T(8,128)(2,1)S(1)} all-to-all(bf16[32,8,8,256]{3,2,1,0:T(8,128)(2,1)S(1)} %pack_both.1), channel_id=1, replica_groups=mesh['region'=8,'member'=32] {'member'}, dimensions={0} | all-to-all | bytes 2097152 | tf_op jit(solution)/shard_map/cond/branch_1_fun/all_to_all | solution.py:302
  39.4 0.3 gram.3
  39.7 16.7 %all_to_all.33.entries = bf16[32,2,8,256]{3,2,1,0:T(8,128)(2,1)S(1)} all-to-all(bf16[32,2,8,256]{3,2,1,0:T(8,128)(2,1)S(1)} %gram.3), channel_id=1, replica_groups=mesh['region'=8,'member'=32] {'member'}, dimensions={0} | all-to-all | bytes 524288 | tf_op jit(solution)/shard_map/cond/branch_1_fun/all_to_all | solution.py:302
  56.4 0.8 combine.1
  57.3 15.3 %all_to_all.34 = bf16[32,2,8,256]{3,2,1,0:T(8,128)(2,1)S(1)} all-to-all(bf16[32,2,8,256]{3,2,1,0:T(8,128)(2,1)S(1)} %get-tuple-element.61), channel_id=1, replica_groups=mesh['region'=8,'member'=32] {'member'}, dimensions={0} | all-to-all | bytes 524288 | tf_op jit(solution)/shard_map/cond/branch_1_fun/all_to_all | solution.py:302
  72.6 2.6 %mix.1 = bf16[32,6,8,256]{3,2,1,0:T(8,128)(2,1)S(1)} custom-call(bf16[32,2,8,256]{3,2,1,0:T(8,128)(2,1)S(1)} %get-tuple-element.69.entries, bf16[2,256,768]{2,1,0:T(8,128)(2,1)S(1)} %get-tuple-element.70.pert, f32[2,8,768]{2,1,0:T(8,128)S(1)} %get-tuple-element.71.centre), custom_call_target="tpu_custom_call" | custom-call | tf_op jit(solution)/shard_map/mix/pallas_call | solution.py:438
  75.1 22.3 %all_to_all.35.parts = bf16[32,6,8,256]{3,2,1,0:T(8,128)(2,1)S(1)} all-to-all(bf16[32,6,8,256]{3,2,1,0:T(8,128)(2,1)S(1)} %mix.1), channel_id=1, replica_groups=mesh['region'=8,'member'=32] {'member'}, dimensions={0} | all-to-all | bytes 1572864 | tf_op jit(solution)/shard_map/all_to_all | solution.py:302
  97.4 0.9 unpack.1
Async XLA Ops:
  0.0 0.7 copy-start
  0.0 7.5 %copy-start.5 = (bf16[8,14336]{1,0:T(8,128)(2,1)S(1)}, bf16[8,14336]{1,0:T(8,128)(2,1)}, u32[]{:S(2)}) copy-start(bf16[8,14336]{1,0:T(8,128)(2,1)} %param.11) | copy-start | bytes 688132
  0.7 6.8 %copy-start.6 = (f32[14336]{0:T(1024)S(1)}, f32[14336]{0:T(1024)}, u32[]{:S(2)}) copy-start(f32[14336]{0:T(1024)} %param.12) | copy-start | bytes 172036
  0.7 6.8 %copy-start.7 = (f32[14336]{0:T(1024)S(1)}, f32[14336]{0:T(1024)}, u32[]{:S(2)}) copy-start(f32[14336]{0:T(1024)} %param.13) | copy-start | bytes 172036
  2.2 5.2 %collective-permute-start = (bf16[8,8,256]{2,1,0:T(8,128)(2,1)S(1)}, bf16[8,8,256]{2,1,0:T(8,128)(2,1)S(1)}, u32[]{:S(2)}, u32[]{:S(2)}) collective-permute-start(bf16[8,8,256]{2,1,0:T(8,128)(2,1)S(1)} %get-tuple-element.67), channel_id=1, source_target_pairs={{32,64},{64,32},{96,128},{128,96},{160,192},{192,160},{33,65},{65,... | collective-permute-start | bytes 98312 | tf_op jit(solution)/shard_map/ppermute | solution.py:298
  4.2 3.3 %collective-permute-start.1 = (bf16[8,8,256]{2,1,0:T(8,128)(2,1)S(1)}, bf16[8,8,256]{2,1,0:T(8,128)(2,1)S(1)}, u32[]{:S(2)}, u32[]{:S(2)}) collective-permute-start(bf16[8,8,256]{2,1,0:T(8,128)(2,1)S(1)} %get-tuple-element.68), channel_id=1, source_target_pairs={{0,32},{32,0},{64,96},{96,64},{128,160},{160,128},{192,224},{224,1... | collective-permute-start | bytes 98312 | tf_op jit(solution)/shard_map/ppermute | solution.py:298
  5.8 0.7 copy-start.2
  5.8 0.7 copy-start.1
  5.8 0.7 copy-start.3

commit v5 on v4

--- a/solution.py
+++ b/solution.py
@@ -44,7 +44,8 @@
 
 
 def product(a, b):
-    return dot(a[0], b[0]) + (dot(a[0], b[1]) + dot(a[1], b[0]))
+    left = jnp.concatenate([a[0], a[0], a[1]], axis=1)
+    return dot(left, jnp.concatenate([b[0], b[1], b[0]], axis=0))
 
 
 def rounded(a):
@@ -160,18 +161,15 @@
     out[:, 0], out[:, 1] = grams_of(*about, gathered, gathered.shape[1] - 2)
 
 
-def pick_kernel(region, chosen, blocks, val, wgt, across, within, vals, wgts, sems):
+def pick_kernel(region, chosen, blocks, val, wgt, across, within, held, vals, wgts, sems):
     odd = region[0] & 1
     sides = ((1 - odd, across), (odd, within))
-    pairs = [(val, vals), (wgt, wgts)]
-    for side, out in sides:
-        for k in range(HANDED):
-            pairs.append((blocks.at[chosen[side, k]], out.at[k]))
-    landed(in_flight(pairs, sems))
+    landed(in_flight([(blocks, held), (val, vals), (wgt, wgts)], sems))
     row = iota((OWN, OBS), 0)
     for side, out in sides:
         for k in range(HANDED):
             block = chosen[side, k]
+            out[k] = held[block]
             w, v = wide_row(wgts[block]), wide_row(vals[block])
             w_high, v_high = rounded(w), rounded(v)
             tail = jnp.where(row == 2, v_high, jnp.where(row == 3, v - v_high, 0.0))
@@ -278,9 +276,10 @@
     z3 = [1.5 * z - 0.5 * product(a, b) for z, a, b in zip(z2, az, zz)]
     for half in range(2):
         spread = z3[half] / jnp.sqrt(bounds[half])
-        inner = jnp.sum(spread * vectors[half], axis=0, keepdims=True)
-        shift = jnp.sum(spread * inner, axis=1, keepdims=True) / (MEMBERS - 1.0)
-        mixing = (spread + shift).T.astype(BF16)
+        across = jnp.sum(eye * vectors[half], axis=0, keepdims=True)
+        inner = jnp.sum(spread * across, axis=1, keepdims=True)
+        shift = jnp.sum(spread * inner, axis=0, keepdims=True) / (MEMBERS - 1.0)
+        mixing = (spread + shift).astype(BF16)
         result = dot(mixing, pert[half]) + centre[half][:1]
         for level in range(LEVELS):
             rows = result[:, level * 128 : (level + 1) * 128].reshape(PEERS, OWN, 128)
@@ -344,9 +343,10 @@
         in_specs=[SCALARS, SCALARS, HBM, HBM, HBM],
         out_specs=(WHOLE, WHOLE),
         scratch_shapes=[
+            pltpu.VMEM((HOME, OWN, OBS), BF16),
             pltpu.VMEM((HOME, 2, 128), F32),
             pltpu.VMEM((HOME, 2, 128), F32),
-            pltpu.SemaphoreType.DMA((2 * HANDED + 2,)),
+            pltpu.SemaphoreType.DMA((3,)),
         ],
         compiler_params=PARAMS,
         name="pick",

time: 98.7 us -> 98.6 us (level)
  no operation moved by 1% of the time
where the time goes in v5:
time: 98.6 us; the launch traced here: 98.2 us
  blocking collectives  84.9 us (86%)
  Pallas kernels  7.96 us (8%)
  starting transfers between devices  3.6 us (4%)
  local copies, waits for them, and re-layouts  1.38 us (1%)
    all_to_all x4, blocking collectives, exchange(): lax.all_to_all(value, 'member', split_axis=0, concat_axis=0, tiled=True)  84.9 us
    ppermute x2, starting transfers between devices, swapped(): return lax.ppermute(value, 'region', pairs)  3.6 us
    pallas_call x1, Pallas kernels, on_device(): pl.pallas_call(mix_kernel, out_shape=shape(PEERS, LEVELS, OWN, COLS), in_...  2.43 us
  transfers between devices with their start and end apart: 2, of which 1 were waited for; matrix products, arithmetic and copies ran while one was open for 0% of the time, Pallas kernels for 1%

profile of v5, /device:TPU:2, one launch (start us, length us, event | category | flops | bytes accessed | tf_op | source)
XLA Modules:
  0.0 98.2 jit_solution(12799297174412570121)
XLA Ops:
  0.0 0.0 copy-start
  0.0 0.0 copy-start.5
  0.0 0.7 copy-done
  0.7 0.0 copy-start.6
  0.7 0.0 copy-start.7
  0.7 1.6 %pick.1 = (bf16[8,8,256]{2,1,0:T(8,128)(2,1)S(1)}, bf16[8,8,256]{2,1,0:T(8,128)(2,1)S(1)}) custom-call(s32[1]{0:T(128)} %bitcast.region, s32[2,4]{1,0:T(2,128)S(1)} %copy-done, bf16[56,8,256]{2,1,0:T(8,128)(2,1)} %bitcast.17, f32[56,2,128]{2,1,0:T(2,128)} %bitcast.20, f32[56,2,128]{2,1,0:T(2,128)} %bitcast.23), custom_call_target="tpu_custom_call" | custom-call | tf_op jit(solution)/shard_map/pick/pallas_call | solution.py:340
  2.3 1.9 %collective-permute-start = (bf16[8,8,256]{2,1,0:T(8,128)(2,1)S(1)}, bf16[8,8,256]{2,1,0:T(8,128)(2,1)S(1)}, u32[]{:S(2)}, u32[]{:S(2)}) collective-permute-start(bf16[8,8,256]{2,1,0:T(8,128)(2,1)S(1)} %get-tuple-element.67), channel_id=1, source_target_pairs={{32,64},{64,32},{96,128},{128,96},{160,192},{192,160},{33,65},{65,... | collective-permute-start | bytes 98312 | tf_op jit(solution)/shard_map/ppermute | solution.py:297
  4.2 1.7 %collective-permute-start.1 = (bf16[8,8,256]{2,1,0:T(8,128)(2,1)S(1)}, bf16[8,8,256]{2,1,0:T(8,128)(2,1)S(1)}, u32[]{:S(2)}, u32[]{:S(2)}) collective-permute-start(bf16[8,8,256]{2,1,0:T(8,128)(2,1)S(1)} %get-tuple-element.68), channel_id=1, source_target_pairs={{0,32},{32,0},{64,96},{96,64},{128,160},{160,128},{192,224},{224,1... | collective-permute-start | bytes 98312 | tf_op jit(solution)/shard_map/ppermute | solution.py:297
  5.9 0.0 copy-start.2
  5.9 0.0 copy-start.1
  5.9 0.0 copy-start.3
  5.9 0.7 copy-done.2
  6.6 0.0 copy-done.1
  6.6 0.0 copy-done.3
  6.6 0.6 lists.1
  7.2 0.3 collective-permute-done
  7.5 0.0 collective-permute-done.1
  7.5 0.0 copy-done.5
  7.5 0.0 copy-done.6
  7.5 0.0 copy-done.7
  7.5 65.1 %conditional.1 = ((bf16[2,256,768]{2,1,0:T(8,128)(2,1)S(1)}, f32[2,8,768]{2,1,0:T(8,128)S(1)}, bf16[32,2,8,256]{3,2,1,0:T(8,128)(2,1)S(1)})) conditional(s32[]{:T(128)} %convert_element_type.3, (s32[1]{0:T(128)}, bf16[28,2,8,256]{3,2,1,0:T(8,128)(2,1)S(1)}, bf16[8,8,256]{2,1,0:T(8,128)(2,1)S(1)}, bf16[8,8,256]{2,1,0:T(8,128)(2,1)S(1)}, s32[1]{0:T(128)}, ...), branch_computations={%region_0.1_spmd, %region_1.2_spmd} | conditional | bytes 6291492 | solution.py:429
  7.5 1.3 %pack_both.1 = bf16[32,8,8,256]{3,2,1,0:T(8,128)(2,1)S(1)} custom-call(s32[1]{0:T(128)} %get-tuple-element.51.region.refs_1_, bf16[6,32,8,256]{3,2,1,0:T(8,128)(2,1)} %get-tuple-element.57.fields, bf16[28,2,8,256]{3,2,1,0:T(8,128)(2,1)S(1)} %get-tuple-element.58.blocks, bf16[8,8,256]{2,1,0:T(8,128)(2,1)S(1)} %get-tuple-element.55.across.refs_5_, ...), custom_call_target="tpu_custom_call" | custom-call | tf_op jit(solution)/shard_map/cond/branch_1_fun/pack_both/pallas_call | solution.py:369
  8.8 30.6 %all_to_all.32.refs_7_.fields = bf16[32,8,8,256]{3,2,1,0:T(8,128)(2,1)S(1)} all-to-all(bf16[32,8,8,256]{3,2,1,0:T(8,128)(2,1)S(1)} %pack_both.1), channel_id=1, replica_groups=mesh['region'=8,'member'=32] {'member'}, dimensions={0} | all-to-all | bytes 2097152 | tf_op jit(solution)/shard_map/cond/branch_1_fun/all_to_all | solution.py:301
  39.5 0.3 gram.3
  39.8 16.7 %all_to_all.33.entries = bf16[32,2,8,256]{3,2,1,0:T(8,128)(2,1)S(1)} all-to-all(bf16[32,2,8,256]{3,2,1,0:T(8,128)(2,1)S(1)} %gram.3), channel_id=1, replica_groups=mesh['region'=8,'member'=32] {'member'}, dimensions={0} | all-to-all | bytes 524288 | tf_op jit(solution)/shard_map/cond/branch_1_fun/all_to_all | solution.py:301
  56.5 0.8 combine.1
  57.3 15.3 %all_to_all.34 = bf16[32,2,8,256]{3,2,1,0:T(8,128)(2,1)S(1)} all-to-all(bf16[32,2,8,256]{3,2,1,0:T(8,128)(2,1)S(1)} %get-tuple-element.61), channel_id=1, replica_groups=mesh['region'=8,'member'=32] {'member'}, dimensions={0} | all-to-all | bytes 524288 | tf_op jit(solution)/shard_map/cond/branch_1_fun/all_to_all | solution.py:301
  72.6 2.4 %mix.1 = bf16[32,6,8,256]{3,2,1,0:T(8,128)(2,1)S(1)} custom-call(bf16[32,2,8,256]{3,2,1,0:T(8,128)(2,1)S(1)} %get-tuple-element.69.entries, bf16[2,256,768]{2,1,0:T(8,128)(2,1)S(1)} %get-tuple-element.70.pert, f32[2,8,768]{2,1,0:T(8,128)S(1)} %get-tuple-element.71.centre), custom_call_target="tpu_custom_call" | custom-call | tf_op jit(solution)/shard_map/mix/pallas_call | solution.py:438
  75.0 22.3 %all_to_all.35.parts = bf16[32,6,8,256]{3,2,1,0:T(8,128)(2,1)S(1)} all-to-all(bf16[32,6,8,256]{3,2,1,0:T(8,128)(2,1)S(1)} %mix.1), channel_id=1, replica_groups=mesh['region'=8,'member'=32] {'member'}, dimensions={0} | all-to-all | bytes 1572864 | tf_op jit(solution)/shard_map/all_to_all | solution.py:301
  97.3 0.9 unpack.1
Async XLA Ops:
  0.0 0.7 copy-start
  0.0 7.5 %copy-start.5 = (bf16[8,14336]{1,0:T(8,128)(2,1)S(1)}, bf16[8,14336]{1,0:T(8,128)(2,1)}, u32[]{:S(2)}) copy-start(bf16[8,14336]{1,0:T(8,128)(2,1)} %param.11) | copy-start | bytes 688132
  0.7 6.8 %copy-start.6 = (f32[14336]{0:T(1024)S(1)}, f32[14336]{0:T(1024)}, u32[]{:S(2)}) copy-start(f32[14336]{0:T(1024)} %param.12) | copy-start | bytes 172036
  0.7 6.8 %copy-start.7 = (f32[14336]{0:T(1024)S(1)}, f32[14336]{0:T(1024)}, u32[]{:S(2)}) copy-start(f32[14336]{0:T(1024)} %param.13) | copy-start | bytes 172036
  2.3 5.2 %collective-permute-start = (bf16[8,8,256]{2,1,0:T(8,128)(2,1)S(1)}, bf16[8,8,256]{2,1,0:T(8,128)(2,1)S(1)}, u32[]{:S(2)}, u32[]{:S(2)}) collective-permute-start(bf16[8,8,256]{2,1,0:T(8,128)(2,1)S(1)} %get-tuple-element.67), channel_id=1, source_target_pairs={{32,64},{64,32},{96,128},{128,96},{160,192},{192,160},{33,65},{65,... | collective-permute-start | bytes 98312 | tf_op jit(solution)/shard_map/ppermute | solution.py:297
  4.2 3.3 %collective-permute-start.1 = (bf16[8,8,256]{2,1,0:T(8,128)(2,1)S(1)}, bf16[8,8,256]{2,1,0:T(8,128)(2,1)S(1)}, u32[]{:S(2)}, u32[]{:S(2)}) collective-permute-start(bf16[8,8,256]{2,1,0:T(8,128)(2,1)S(1)} %get-tuple-element.68), channel_id=1, source_target_pairs={{0,32},{32,0},{64,96},{96,64},{128,160},{160,128},{192,224},{224,1... | collective-permute-start | bytes 98312 | tf_op jit(solution)/shard_map/ppermute | solution.py:297
  5.9 0.7 copy-start.2
  5.9 0.7 copy-start.1
  5.9 0.7 copy-start.3

commit v6 on v5

--- a/solution.py
+++ b/solution.py
@@ -41,6 +41,10 @@
 def split(a):
     high = a.astype(BF16)
     return high, (a - high.astype(F32)).astype(BF16)
+
+
+def single(a, b):
+    return dot(a.astype(BF16), b.astype(BF16))
 
 
 def product(a, b):
@@ -262,10 +266,9 @@
         bounds.append(bound)
         a1.append(system / bound)
     s1 = [split(a) for a in a1]
-    a2 = [product(s, s) for s in s1]
-    s2 = [split(a) for a in a2]
-    a3 = [product(s, t) for s, t in zip(s2, s1)]
-    a4 = [product(s, s) for s in s2]
+    a2 = [single(a, a) for a in a1]
+    a3 = [single(a, b) for a, b in zip(a2, a1)]
+    a4 = [single(a, a) for a in a2]
     z2 = [
         2.25 * eye - 2.4375 * a + 1.6875 * b - 0.5625 * c + 0.0625 * d
         for a, b, c, d in zip(a1, a2, a3, a4)

time: 98.6 us -> 98.1 us (level)
  no operation moved by 1% of the time
where the time goes in v6:
time: 98.1 us; the launch traced here: 97.8 us
  blocking collectives  84.9 us (87%)
  Pallas kernels  7.53 us (8%)
  starting transfers between devices  3.6 us (4%)
  local copies, waits for them, and re-layouts  1.38 us (1%)
    all_to_all x4, blocking collectives, exchange(): lax.all_to_all(value, 'member', split_axis=0, concat_axis=0, tiled=True)  84.9 us
    ppermute x2, starting transfers between devices, swapped(): return lax.ppermute(value, 'region', pairs)  3.6 us
    pallas_call x1, Pallas kernels, on_device(): pl.pallas_call(mix_kernel, out_shape=shape(PEERS, LEVELS, OWN, COLS), in_...  2 us
  transfers between devices with their start and end apart: 2, of which 1 were waited for; matrix products, arithmetic and copies ran while one was open for 0% of the time, Pallas kernels for 1%

profile of v6, /device:TPU:2, one launch (start us, length us, event | category | flops | bytes accessed | tf_op | source)
XLA Modules:
  0.0 97.8 jit_solution(13965797941983561679)
XLA Ops:
  0.0 0.0 copy-start
  0.0 0.0 copy-start.5
  0.0 0.7 copy-done
  0.7 0.0 copy-start.6
  0.7 0.0 copy-start.7
  0.7 1.6 %pick.1 = (bf16[8,8,256]{2,1,0:T(8,128)(2,1)S(1)}, bf16[8,8,256]{2,1,0:T(8,128)(2,1)S(1)}) custom-call(s32[1]{0:T(128)} %bitcast.region, s32[2,4]{1,0:T(2,128)S(1)} %copy-done, bf16[56,8,256]{2,1,0:T(8,128)(2,1)} %bitcast.17, f32[56,2,128]{2,1,0:T(2,128)} %bitcast.20, f32[56,2,128]{2,1,0:T(2,128)} %bitcast.23), custom_call_target="tpu_custom_call" | custom-call | tf_op jit(solution)/shard_map/pick/pallas_call | solution.py:343
  2.3 1.9 %collective-permute-start = (bf16[8,8,256]{2,1,0:T(8,128)(2,1)S(1)}, bf16[8,8,256]{2,1,0:T(8,128)(2,1)S(1)}, u32[]{:S(2)}, u32[]{:S(2)}) collective-permute-start(bf16[8,8,256]{2,1,0:T(8,128)(2,1)S(1)} %get-tuple-element.67), channel_id=1, source_target_pairs={{32,64},{64,32},{96,128},{128,96},{160,192},{192,160},{33,65},{65,... | collective-permute-start | bytes 98312 | tf_op jit(solution)/shard_map/ppermute | solution.py:300
  4.2 1.7 %collective-permute-start.1 = (bf16[8,8,256]{2,1,0:T(8,128)(2,1)S(1)}, bf16[8,8,256]{2,1,0:T(8,128)(2,1)S(1)}, u32[]{:S(2)}, u32[]{:S(2)}) collective-permute-start(bf16[8,8,256]{2,1,0:T(8,128)(2,1)S(1)} %get-tuple-element.68), channel_id=1, source_target_pairs={{0,32},{32,0},{64,96},{96,64},{128,160},{160,128},{192,224},{224,1... | collective-permute-start | bytes 98312 | tf_op jit(solution)/shard_map/ppermute | solution.py:300
  5.9 0.0 copy-start.2
  5.9 0.0 copy-start.1
  5.9 0.0 copy-start.3
  5.9 0.7 copy-done.2
  6.6 0.0 copy-done.1
  6.6 0.0 copy-done.3
  6.6 0.6 lists.1
  7.2 0.3 collective-permute-done
  7.5 0.0 collective-permute-done.1
  7.5 0.0 copy-done.5
  7.5 0.0 copy-done.6
  7.5 0.0 copy-done.7
  7.5 65.1 %conditional.1 = ((bf16[2,256,768]{2,1,0:T(8,128)(2,1)S(1)}, f32[2,8,768]{2,1,0:T(8,128)S(1)}, bf16[32,2,8,256]{3,2,1,0:T(8,128)(2,1)S(1)})) conditional(s32[]{:T(128)} %convert_element_type.3, (s32[1]{0:T(128)}, bf16[28,2,8,256]{3,2,1,0:T(8,128)(2,1)S(1)}, bf16[8,8,256]{2,1,0:T(8,128)(2,1)S(1)}, bf16[8,8,256]{2,1,0:T(8,128)(2,1)S(1)}, s32[1]{0:T(128)}, ...), branch_computations={%region_0.1_spmd, %region_1.2_spmd} | conditional | bytes 6291492 | solution.py:432
  7.5 1.3 %pack_both.1 = bf16[32,8,8,256]{3,2,1,0:T(8,128)(2,1)S(1)} custom-call(s32[1]{0:T(128)} %get-tuple-element.51.region.refs_1_, bf16[6,32,8,256]{3,2,1,0:T(8,128)(2,1)} %get-tuple-element.57.fields, bf16[28,2,8,256]{3,2,1,0:T(8,128)(2,1)S(1)} %get-tuple-element.58.blocks, bf16[8,8,256]{2,1,0:T(8,128)(2,1)S(1)} %get-tuple-element.55.across.refs_5_, ...), custom_call_target="tpu_custom_call" | custom-call | tf_op jit(solution)/shard_map/cond/branch_1_fun/pack_both/pallas_call | solution.py:372
  8.8 30.6 %all_to_all.32.refs_7_.fields = bf16[32,8,8,256]{3,2,1,0:T(8,128)(2,1)S(1)} all-to-all(bf16[32,8,8,256]{3,2,1,0:T(8,128)(2,1)S(1)} %pack_both.1), channel_id=1, replica_groups=mesh['region'=8,'member'=32] {'member'}, dimensions={0} | all-to-all | bytes 2097152 | tf_op jit(solution)/shard_map/cond/branch_1_fun/all_to_all | solution.py:304
  39.5 0.3 gram.3
  39.8 16.7 %all_to_all.33.entries = bf16[32,2,8,256]{3,2,1,0:T(8,128)(2,1)S(1)} all-to-all(bf16[32,2,8,256]{3,2,1,0:T(8,128)(2,1)S(1)} %gram.3), channel_id=1, replica_groups=mesh['region'=8,'member'=32] {'member'}, dimensions={0} | all-to-all | bytes 524288 | tf_op jit(solution)/shard_map/cond/branch_1_fun/all_to_all | solution.py:304
  56.5 0.8 combine.1
  57.3 15.3 %all_to_all.34 = bf16[32,2,8,256]{3,2,1,0:T(8,128)(2,1)S(1)} all-to-all(bf16[32,2,8,256]{3,2,1,0:T(8,128)(2,1)S(1)} %get-tuple-element.61), channel_id=1, replica_groups=mesh['region'=8,'member'=32] {'member'}, dimensions={0} | all-to-all | bytes 524288 | tf_op jit(solution)/shard_map/cond/branch_1_fun/all_to_all | solution.py:304
  72.6 2.0 %mix.1 = bf16[32,6,8,256]{3,2,1,0:T(8,128)(2,1)S(1)} custom-call(bf16[32,2,8,256]{3,2,1,0:T(8,128)(2,1)S(1)} %get-tuple-element.69.entries, bf16[2,256,768]{2,1,0:T(8,128)(2,1)S(1)} %get-tuple-element.70.pert, f32[2,8,768]{2,1,0:T(8,128)S(1)} %get-tuple-element.71.centre), custom_call_target="tpu_custom_call" | custom-call | tf_op jit(solution)/shard_map/mix/pallas_call | solution.py:441
  74.6 22.3 %all_to_all.35.parts = bf16[32,6,8,256]{3,2,1,0:T(8,128)(2,1)S(1)} all-to-all(bf16[32,6,8,256]{3,2,1,0:T(8,128)(2,1)S(1)} %mix.1), channel_id=1, replica_groups=mesh['region'=8,'member'=32] {'member'}, dimensions={0} | all-to-all | bytes 1572864 | tf_op jit(solution)/shard_map/all_to_all | solution.py:304
  96.9 0.9 unpack.1
Async XLA Ops:
  0.0 0.7 copy-start
  0.0 7.5 %copy-start.5 = (bf16[8,14336]{1,0:T(8,128)(2,1)S(1)}, bf16[8,14336]{1,0:T(8,128)(2,1)}, u32[]{:S(2)}) copy-start(bf16[8,14336]{1,0:T(8,128)(2,1)} %param.11) | copy-start | bytes 688132
  0.7 6.8 %copy-start.6 = (f32[14336]{0:T(1024)S(1)}, f32[14336]{0:T(1024)}, u32[]{:S(2)}) copy-start(f32[14336]{0:T(1024)} %param.12) | copy-start | bytes 172036
  0.7 6.8 %copy-start.7 = (f32[14336]{0:T(1024)S(1)}, f32[14336]{0:T(1024)}, u32[]{:S(2)}) copy-start(f32[14336]{0:T(1024)} %param.13) | copy-start | bytes 172036
  2.3 5.2 %collective-permute-start = (bf16[8,8,256]{2,1,0:T(8,128)(2,1)S(1)}, bf16[8,8,256]{2,1,0:T(8,128)(2,1)S(1)}, u32[]{:S(2)}, u32[]{:S(2)}) collective-permute-start(bf16[8,8,256]{2,1,0:T(8,128)(2,1)S(1)} %get-tuple-element.67), channel_id=1, source_target_pairs={{32,64},{64,32},{96,128},{128,96},{160,192},{192,160},{33,65},{65,... | collective-permute-start | bytes 98312 | tf_op jit(solution)/shard_map/ppermute | solution.py:300
  4.2 3.3 %collective-permute-start.1 = (bf16[8,8,256]{2,1,0:T(8,128)(2,1)S(1)}, bf16[8,8,256]{2,1,0:T(8,128)(2,1)S(1)}, u32[]{:S(2)}, u32[]{:S(2)}) collective-permute-start(bf16[8,8,256]{2,1,0:T(8,128)(2,1)S(1)} %get-tuple-element.68), channel_id=1, source_target_pairs={{0,32},{32,0},{64,96},{96,64},{128,160},{160,128},{192,224},{224,1... | collective-permute-start | bytes 98312 | tf_op jit(solution)/shard_map/ppermute | solution.py:300
  5.9 0.7 copy-start.2
  5.9 0.7 copy-start.1
  5.9 0.7 copy-start.3

commit v7 on v6

--- a/solution.py
+++ b/solution.py
@@ -265,17 +265,16 @@
         bound = jnp.max(sums, axis=0, keepdims=True)
         bounds.append(bound)
         a1.append(system / bound)
-    s1 = [split(a) for a in a1]
     a2 = [single(a, a) for a in a1]
     a3 = [single(a, b) for a, b in zip(a2, a1)]
     a4 = [single(a, a) for a in a2]
-    z2 = [
-        2.25 * eye - 2.4375 * a + 1.6875 * b - 0.5625 * c + 0.0625 * d
+    w = [
+        2.4375 * a - 1.6875 * b + 0.5625 * c - 0.0625 * d
         for a, b, c, d in zip(a1, a2, a3, a4)
     ]
-    t2 = [split(z) for z in z2]
-    az = [split(product(s, t)) for s, t in zip(s1, t2)]
-    zz = [split(product(t, t)) for t in t2]
+    z2 = [2.25 * eye - d for d in w]
+    az = [split(2.25 * a - single(a, d)) for a, d in zip(a1, w)]
+    zz = [split(5.0625 * eye - 4.5 * d + single(d, d)) for d in w]
     z3 = [1.5 * z - 0.5 * product(a, b) for z, a, b in zip(z2, az, zz)]
     for half in range(2):
         spread = z3[half] / jnp.sqrt(bounds[half])

time: 98.1 us -> 97.9 us (level)
  no operation moved by 1% of the time
where the time goes in v7:
time: 97.9 us; the launch traced here: 97.5 us
  blocking collectives  84.9 us (87%)
  Pallas kernels  7.26 us (7%)
  starting transfers between devices  3.6 us (4%)
  local copies, waits for them, and re-layouts  1.38 us (1%)
    all_to_all x4, blocking collectives, exchange(): lax.all_to_all(value, 'member', split_axis=0, concat_axis=0, tiled=True)  84.9 us
    ppermute x2, starting transfers between devices, swapped(): return lax.ppermute(value, 'region', pairs)  3.6 us
  transfers between devices with their start and end apart: 2, of which 1 were waited for; matrix products, arithmetic and copies ran while one was open for 0% of the time, Pallas kernels for 1%

profile of v7, /device:TPU:2, one launch (start us, length us, event | category | flops | bytes accessed | tf_op | source)
XLA Modules:
  0.0 97.5 jit_solution(16134102076138034679)
XLA Ops:
  0.0 0.0 copy-start
  0.0 0.0 copy-start.5
  0.0 0.7 copy-done
  0.7 0.0 copy-start.6
  0.7 0.0 copy-start.7
  0.7 1.6 %pick.1 = (bf16[8,8,256]{2,1,0:T(8,128)(2,1)S(1)}, bf16[8,8,256]{2,1,0:T(8,128)(2,1)S(1)}) custom-call(s32[1]{0:T(128)} %bitcast.region, s32[2,4]{1,0:T(2,128)S(1)} %copy-done, bf16[56,8,256]{2,1,0:T(8,128)(2,1)} %bitcast.17, f32[56,2,128]{2,1,0:T(2,128)} %bitcast.20, f32[56,2,128]{2,1,0:T(2,128)} %bitcast.23), custom_call_target="tpu_custom_call" | custom-call | tf_op jit(solution)/shard_map/pick/pallas_call | solution.py:342
  2.3 1.9 %collective-permute-start = (bf16[8,8,256]{2,1,0:T(8,128)(2,1)S(1)}, bf16[8,8,256]{2,1,0:T(8,128)(2,1)S(1)}, u32[]{:S(2)}, u32[]{:S(2)}) collective-permute-start(bf16[8,8,256]{2,1,0:T(8,128)(2,1)S(1)} %get-tuple-element.67), channel_id=1, source_target_pairs={{32,64},{64,32},{96,128},{128,96},{160,192},{192,160},{33,65},{65,... | collective-permute-start | bytes 98312 | tf_op jit(solution)/shard_map/ppermute | solution.py:299
  4.2 1.7 %collective-permute-start.1 = (bf16[8,8,256]{2,1,0:T(8,128)(2,1)S(1)}, bf16[8,8,256]{2,1,0:T(8,128)(2,1)S(1)}, u32[]{:S(2)}, u32[]{:S(2)}) collective-permute-start(bf16[8,8,256]{2,1,0:T(8,128)(2,1)S(1)} %get-tuple-element.68), channel_id=1, source_target_pairs={{0,32},{32,0},{64,96},{96,64},{128,160},{160,128},{192,224},{224,1... | collective-permute-start | bytes 98312 | tf_op jit(solution)/shard_map/ppermute | solution.py:299
  5.9 0.0 copy-start.2
  5.9 0.0 copy-start.1
  5.9 0.0 copy-start.3
  5.9 0.7 copy-done.2
  6.6 0.0 copy-done.1
  6.6 0.0 copy-done.3
  6.6 0.6 lists.1
  7.2 0.3 collective-permute-done
  7.5 0.0 collective-permute-done.1
  7.5 0.0 copy-done.5
  7.5 0.0 copy-done.6
  7.5 0.0 copy-done.7
  7.5 65.1 %conditional.1 = ((bf16[2,256,768]{2,1,0:T(8,128)(2,1)S(1)}, f32[2,8,768]{2,1,0:T(8,128)S(1)}, bf16[32,2,8,256]{3,2,1,0:T(8,128)(2,1)S(1)})) conditional(s32[]{:T(128)} %convert_element_type.3, (s32[1]{0:T(128)}, bf16[28,2,8,256]{3,2,1,0:T(8,128)(2,1)S(1)}, bf16[8,8,256]{2,1,0:T(8,128)(2,1)S(1)}, bf16[8,8,256]{2,1,0:T(8,128)(2,1)S(1)}, s32[1]{0:T(128)}, ...), branch_computations={%region_0.1_spmd, %region_1.2_spmd} | conditional | bytes 6291492 | solution.py:431
  7.5 1.3 %pack_both.1 = bf16[32,8,8,256]{3,2,1,0:T(8,128)(2,1)S(1)} custom-call(s32[1]{0:T(128)} %get-tuple-element.51.region.refs_1_, bf16[6,32,8,256]{3,2,1,0:T(8,128)(2,1)} %get-tuple-element.57.fields, bf16[28,2,8,256]{3,2,1,0:T(8,128)(2,1)S(1)} %get-tuple-element.58.blocks, bf16[8,8,256]{2,1,0:T(8,128)(2,1)S(1)} %get-tuple-element.55.across.refs_5_, ...), custom_call_target="tpu_custom_call" | custom-call | tf_op jit(solution)/shard_map/cond/branch_1_fun/pack_both/pallas_call | solution.py:371
  8.8 30.6 %all_to_all.32.refs_7_.fields = bf16[32,8,8,256]{3,2,1,0:T(8,128)(2,1)S(1)} all-to-all(bf16[32,8,8,256]{3,2,1,0:T(8,128)(2,1)S(1)} %pack_both.1), channel_id=1, replica_groups=mesh['region'=8,'member'=32] {'member'}, dimensions={0} | all-to-all | bytes 2097152 | tf_op jit(solution)/shard_map/cond/branch_1_fun/all_to_all | solution.py:303
  39.5 0.3 gram.3
  39.8 16.7 %all_to_all.33.entries = bf16[32,2,8,256]{3,2,1,0:T(8,128)(2,1)S(1)} all-to-all(bf16[32,2,8,256]{3,2,1,0:T(8,128)(2,1)S(1)} %gram.3), channel_id=1, replica_groups=mesh['region'=8,'member'=32] {'member'}, dimensions={0} | all-to-all | bytes 524288 | tf_op jit(solution)/shard_map/cond/branch_1_fun/all_to_all | solution.py:303
  56.5 0.8 combine.1
  57.3 15.3 %all_to_all.34 = bf16[32,2,8,256]{3,2,1,0:T(8,128)(2,1)S(1)} all-to-all(bf16[32,2,8,256]{3,2,1,0:T(8,128)(2,1)S(1)} %get-tuple-element.61), channel_id=1, replica_groups=mesh['region'=8,'member'=32] {'member'}, dimensions={0} | all-to-all | bytes 524288 | tf_op jit(solution)/shard_map/cond/branch_1_fun/all_to_all | solution.py:303
  72.6 1.7 %mix.1 = bf16[32,6,8,256]{3,2,1,0:T(8,128)(2,1)S(1)} custom-call(bf16[32,2,8,256]{3,2,1,0:T(8,128)(2,1)S(1)} %get-tuple-element.69.entries, bf16[2,256,768]{2,1,0:T(8,128)(2,1)S(1)} %get-tuple-element.70.pert, f32[2,8,768]{2,1,0:T(8,128)S(1)} %get-tuple-element.71.centre), custom_call_target="tpu_custom_call" | custom-call | tf_op jit(solution)/shard_map/mix/pallas_call | solution.py:440
  74.3 22.3 %all_to_all.35.parts = bf16[32,6,8,256]{3,2,1,0:T(8,128)(2,1)S(1)} all-to-all(bf16[32,6,8,256]{3,2,1,0:T(8,128)(2,1)S(1)} %mix.1), channel_id=1, replica_groups=mesh['region'=8,'member'=32] {'member'}, dimensions={0} | all-to-all | bytes 1572864 | tf_op jit(solution)/shard_map/all_to_all | solution.py:303
  96.6 0.9 unpack.1
Async XLA Ops:
  0.0 0.7 copy-start
  0.0 7.5 %copy-start.5 = (bf16[8,14336]{1,0:T(8,128)(2,1)S(1)}, bf16[8,14336]{1,0:T(8,128)(2,1)}, u32[]{:S(2)}) copy-start(bf16[8,14336]{1,0:T(8,128)(2,1)} %param.11) | copy-start | bytes 688132
  0.7 6.8 %copy-start.6 = (f32[14336]{0:T(1024)S(1)}, f32[14336]{0:T(1024)}, u32[]{:S(2)}) copy-start(f32[14336]{0:T(1024)} %param.12) | copy-start | bytes 172036
  0.7 6.8 %copy-start.7 = (f32[14336]{0:T(1024)S(1)}, f32[14336]{0:T(1024)}, u32[]{:S(2)}) copy-start(f32[14336]{0:T(1024)} %param.13) | copy-start | bytes 172036
  2.3 5.2 %collective-permute-start = (bf16[8,8,256]{2,1,0:T(8,128)(2,1)S(1)}, bf16[8,8,256]{2,1,0:T(8,128)(2,1)S(1)}, u32[]{:S(2)}, u32[]{:S(2)}) collective-permute-start(bf16[8,8,256]{2,1,0:T(8,128)(2,1)S(1)} %get-tuple-element.67), channel_id=1, source_target_pairs={{32,64},{64,32},{96,128},{128,96},{160,192},{192,160},{33,65},{65,... | collective-permute-start | bytes 98312 | tf_op jit(solution)/shard_map/ppermute | solution.py:299
  4.2 3.3 %collective-permute-start.1 = (bf16[8,8,256]{2,1,0:T(8,128)(2,1)S(1)}, bf16[8,8,256]{2,1,0:T(8,128)(2,1)S(1)}, u32[]{:S(2)}, u32[]{:S(2)}) collective-permute-start(bf16[8,8,256]{2,1,0:T(8,128)(2,1)S(1)} %get-tuple-element.68), channel_id=1, source_target_pairs={{0,32},{32,0},{64,96},{96,64},{128,160},{160,128},{192,224},{224,1... | collective-permute-start | bytes 98312 | tf_op jit(solution)/shard_map/ppermute | solution.py:299
  5.9 0.7 copy-start.2
  5.9 0.7 copy-start.1
  5.9 0.7 copy-start.3

commit v8 on v6

--- a/solution.py
+++ b/solution.py
@@ -1,3 +1,5 @@
+import functools
+
 import jax
 import jax.numpy as jnp
 from jax import lax
@@ -22,6 +24,8 @@
 ANY = pl.BlockSpec(memory_space=pl.ANY)
 HBM = pl.BlockSpec(memory_space=pltpu.HBM)
 SCALARS = pl.BlockSpec(memory_space=pltpu.SMEM)
+EVEN = (5, 1, 0)
+ODD = (0, 0, 6)
 PARAMS = pltpu.CompilerParams(vmem_limit_bytes=VMEM_BYTES)
 
 
@@ -86,19 +90,30 @@
     ]
 
 
-def field_pairs(fields, out):
-    return [(fields.at[level], out.at[:, level]) for level in range(LEVELS)]
-
-
-def pack_both_kernel(region, fields, blocks, across, within, out, slots, sems, field_sems):
-    first = in_flight(field_pairs(fields, out), field_sems)
-    pairs = block_pairs(region, blocks, across, within, slots, out, LEVELS)
-    landed(first + in_flight(pairs, sems))
-
-
-def pack_blocks_kernel(region, blocks, across, within, out, slots, sems):
-    pairs = block_pairs(region, blocks, across, within, slots, out, 0)
-    landed(in_flight(pairs, sems))
+def field_pairs(fields, out, levels):
+    return [(fields.at[level], out.at[:, place]) for place, level in enumerate(levels)]
+
+
+def pack_kernel(levels, region, fields, blocks, across, within, out, slots, sems):
+    first = in_flight(field_pairs(fields, out, levels), sems)
+    pairs = block_pairs(region, blocks, across, within, slots, out, len(levels))
+    last = [
+        pltpu.make_async_copy(*ends, sems.at[LEVELS + k]) for k, ends in enumerate(pairs)
+    ]
+    for copy in last:
+        copy.start()
+    landed(first + last)
+
+
+def emit(levels, parts, fields, out, part, sems):
+    if not levels:
+        out[:, 0], out[:, 1] = parts()
+        return
+    copies = in_flight(field_pairs(fields, out, levels), sems)
+    part[:, 0], part[:, 1] = parts()
+    last = pltpu.make_async_copy(part, out.at[:, pl.ds(len(levels), 2)], sems.at[LEVELS])
+    last.start()
+    landed(copies + [last])
 
 
 def first_half(rows):
@@ -160,9 +175,10 @@
     return interleaved(*top).astype(BF16), interleaved(*low).astype(BF16)
 
 
-def gram_kernel(*refs):
-    *about, gathered, out = refs
-    out[:, 0], out[:, 1] = grams_of(*about, gathered, gathered.shape[1] - 2)
+def gram_kernel(levels, *refs):
+    *about, gathered, fields, out, part, sems = refs
+    group = gathered.shape[1] - 2
+    emit(levels, lambda: grams_of(*about, gathered, group), fields, out, part, sems)
 
 
 def pick_kernel(region, chosen, blocks, val, wgt, across, within, held, vals, wgts, sems):
@@ -216,33 +232,34 @@
     return (rows.reshape(PEERS, 8, 256).astype(BF16) for rows in (total[0], tail))
 
 
-def combine_kernel(entries, fields, out, pert, centre):
-    centre_kernel(fields, pert, centre)
-    out[:, 0], out[:, 1] = sums_of(entries[...].astype(F32))
-
-
-def combine_and_pack_kernel(entries, fields, out, part, sems):
-    copies = in_flight(field_pairs(fields, out), sems)
-    part[:, 0], part[:, 1] = sums_of(entries[...].astype(F32))
-    last = pltpu.make_async_copy(part, out.at[:, pl.ds(LEVELS, 2)], sems.at[LEVELS])
-    last.start()
-    landed(copies)
-    last.wait()
-
-
-def centre_kernel(fields, pert, centre, entries=None):
-    if entries is not None:
-        entries[...] = fields[:, LEVELS:]
-    for level in range(LEVELS):
-        x = fields[:, level].astype(F32).reshape(MEMBERS, COLS)
-        mean = jnp.sum(x, axis=0, keepdims=True) / MEMBERS
-        away = (x - mean).astype(BF16)
-        for half in range(2):
-            at = slice(level * 128, (level + 1) * 128)
-            pert[half, :, at] = away[:, half * 128 : (half + 1) * 128]
-            centre[half, :, at] = jnp.broadcast_to(
-                mean[:, half * 128 : (half + 1) * 128], (8, 128)
-            )
+def combine_kernel(levels, earlier, entries, fields, *refs):
+    if levels:
+        out, part, sems = refs
+    else:
+        *sources, out, pert, centre, part, sems = refs
+        centre_of(earlier, [entries if ref is None else ref for ref in sources], pert, centre)
+    group = entries.shape[1] - 2
+    emit(levels, lambda: sums_of(entries[:, group:].astype(F32)), fields, out, part, sems)
+
+
+def centre_of(earlier, sources, pert, centre):
+    for levels, fields in zip(earlier, sources):
+        for place, level in enumerate(levels):
+            x = fields[:, place].astype(F32).reshape(MEMBERS, COLS)
+            mean = jnp.sum(x, axis=0, keepdims=True) / MEMBERS
+            away = (x - mean).astype(BF16)
+            for half in range(2):
+                at = slice(level * 128, (level + 1) * 128)
+                pert[half, :, at] = away[:, half * 128 : (half + 1) * 128]
+                centre[half, :, at] = jnp.broadcast_to(
+                    mean[:, half * 128 : (half + 1) * 128], (8, 128)
+                )
+
+
+def last_kernel(earlier, *refs):
+    *sources, pert, centre, systems = refs
+    centre_of(earlier, sources, pert, centre)
+    systems[...] = sources[-1][:, len(earlier[-1]) :]
 
 
 def mix_kernel(entries, pert, centre, out):
@@ -311,9 +328,6 @@
 CENTRED = (shape(2, MEMBERS, LEVELS * 128), shape(2, 8, LEVELS * 128, dtype=F32))
 
 
-WITH_FIELDS = [pltpu.VMEM((PEERS, 2, 8, 256), BF16), pltpu.SemaphoreType.DMA((LEVELS + 1,))]
-
-
 def on_device(
     background_trajectories,
     sensor_spread_matrix,
@@ -357,82 +371,82 @@
     across = swapped(across, 1)
     within = swapped(within, 0)
 
-    def gram(gathered, *about):
-        return pl.pallas_call(
-            gram_kernel,
-            out_shape=shape(PEERS, 2, 8, 256),
-            in_specs=[SCALARS] * 2 + [WHOLE] * 6,
-            out_specs=WHOLE,
-            compiler_params=PARAMS,
-            name="gram",
-        )(*about, gathered)
-
-    def fields_first(fields, blocks, *about):
+    def chain(split, fields, blocks, *about):
         _, region, *_, across, within = about
+        share = []
+        for count in split:
+            start = sum(len(levels) for levels in share)
+            share.append(tuple(range(start, start + count)))
+        scratch = [
+            pltpu.VMEM((PEERS, 2, 8, 256), BF16),
+            pltpu.SemaphoreType.DMA((LEVELS + 1,)),
+        ]
         packed = pl.pallas_call(
-            pack_both_kernel,
-            out_shape=shape(PEERS, LEVELS + 2, OWN, COLS),
+            functools.partial(pack_kernel, share[0]),
+            out_shape=shape(PEERS, len(share[0]) + 2, OWN, COLS),
             in_specs=[SCALARS, HBM, HBM, WHOLE, WHOLE],
             out_specs=ANY,
             scratch_shapes=[
                 pltpu.VMEM((HANDED, 2, OWN, COLS), BF16),
-                pltpu.SemaphoreType.DMA((2,)),
-                pltpu.SemaphoreType.DMA((LEVELS,)),
+                pltpu.SemaphoreType.DMA((LEVELS + 2,)),
             ],
             compiler_params=PARAMS,
-            name="pack_both",
+            name="pack",
         )(region, fields, blocks, across, within)
         gathered = exchange(packed)
-        grams = exchange(gram(gathered, *about))
-        sums, pert, centre = pl.pallas_call(
-            combine_kernel,
-            out_shape=(shape(PEERS, 2, 8, 256),) + CENTRED,
-            in_specs=[WHOLE] * 2,
+        grams = pl.pallas_call(
+            functools.partial(gram_kernel, share[1]),
+            out_shape=shape(PEERS, len(share[1]) + 2, 8, 256),
+            in_specs=[SCALARS] * 2 + [WHOLE] * 6 + [HBM],
+            out_specs=ANY if share[1] else WHOLE,
+            scratch_shapes=scratch,
+            compiler_params=PARAMS,
+            name="gram",
+        )(*about, gathered, fields)
+        entries = exchange(grams)
+        come = [
+            (levels, array)
+            for levels, array in zip(share, (gathered, entries))
+            if levels
+        ]
+        if not share[2]:
+            earlier = [levels for levels, _ in come]
+            sums, pert, centre = pl.pallas_call(
+                functools.partial(combine_kernel, (), earlier),
+                out_shape=(shape(PEERS, 2, 8, 256),) + CENTRED,
+                in_specs=[WHOLE, HBM] + [WHOLE] * len(come),
+                out_specs=(WHOLE,) * 3,
+                scratch_shapes=scratch,
+                compiler_params=PARAMS,
+                name="combine",
+            )(entries, fields, *(array for _, array in come))
+            return pert, centre, exchange(sums)
+        sums = pl.pallas_call(
+            functools.partial(combine_kernel, share[2], ()),
+            out_shape=shape(PEERS, len(share[2]) + 2, 8, 256),
+            in_specs=[WHOLE, HBM],
+            out_specs=ANY,
+            scratch_shapes=scratch,
+            compiler_params=PARAMS,
+            name="combine",
+        )(entries, fields)
+        come.append((share[2], exchange(sums)))
+        earlier = [levels for levels, _ in come]
+        return pl.pallas_call(
+            functools.partial(last_kernel, earlier),
+            out_shape=CENTRED + (shape(PEERS, 2, 8, 256),),
+            in_specs=[WHOLE] * len(come),
             out_specs=(WHOLE,) * 3,
             compiler_params=PARAMS,
-            name="combine",
-        )(grams, gathered)
-        return pert, centre, exchange(sums)
-
-    def fields_last(fields, blocks, *about):
-        _, region, *_, across, within = about
-        packed = pl.pallas_call(
-            pack_blocks_kernel,
-            out_shape=shape(PEERS, 2, OWN, COLS),
-            in_specs=[SCALARS, HBM, WHOLE, WHOLE],
-            out_specs=ANY,
-            scratch_shapes=[
-                pltpu.VMEM((HANDED, 2, OWN, COLS), BF16),
-                pltpu.SemaphoreType.DMA((2,)),
-            ],
-            compiler_params=PARAMS,
-            name="pack_blocks",
-        )(region, blocks, across, within)
-        grams = exchange(gram(exchange(packed), *about))
-        sums = pl.pallas_call(
-            combine_and_pack_kernel,
-            out_shape=shape(PEERS, LEVELS + 2, OWN, COLS),
-            in_specs=[WHOLE, HBM],
-            out_specs=ANY,
-            scratch_shapes=WITH_FIELDS,
-            compiler_params=PARAMS,
-            name="combine_and_pack",
-        )(grams, fields)
-        return pl.pallas_call(
-            centre_kernel,
-            out_shape=CENTRED + (shape(PEERS, 2, 8, 256),),
-            in_specs=[WHOLE],
-            out_specs=(WHOLE,) * 3,
-            compiler_params=PARAMS,
-            name="centre_and_part",
-        )(exchange(sums))
+            name="centre",
+        )(*(array for _, array in come))
 
     even = lax.axis_index("region") % 2 == 0
     about = (me, region, lists, val, wgt, across, within)
     pert, centre, systems = lax.cond(
         even,
-        fields_first,
-        fields_last,
+        functools.partial(chain, EVEN),
+        functools.partial(chain, ODD),
         fields,
         blocks.reshape(HOME // 2, 2, OWN, OBS),
         *about,

time: 98.1 us -> 98 us (level)
  no operation moved by 1% of the time
where the time goes in v8:
time: 98 us; the launch traced here: 97.7 us
  blocking collectives  84.6 us (86%)
  Pallas kernels  7.67 us (8%)
  starting transfers between devices  3.6 us (4%)
  local copies, waits for them, and re-layouts  1.39 us (1%)
    all_to_all x4, blocking collectives, exchange(): lax.all_to_all(value, 'member', split_axis=0, concat_axis=0, tiled=True)  84.6 us
    ppermute x2, starting transfers between devices, swapped(): return lax.ppermute(value, 'region', pairs)  3.6 us
    pallas_call x1, Pallas kernels, on_device(): pl.pallas_call(mix_kernel, out_shape=shape(PEERS, LEVELS, OWN, COLS), in_...  2 us
  transfers between devices with their start and end apart: 2, of which 1 were waited for; matrix products, arithmetic and copies ran while one was open for 0% of the time, Pallas kernels for 1%

profile of v8, /device:TPU:2, one launch (start us, length us, event | category | flops | bytes accessed | tf_op | source)
XLA Modules:
  0.0 97.7 jit_solution(8348609832484057237)
XLA Ops:
  0.0 0.0 copy-start
  0.0 0.0 copy-start.6
  0.0 0.7 copy-done
  0.7 0.0 copy-start.7
  0.7 0.0 copy-start.8
  0.7 1.6 %pick.1 = (bf16[8,8,256]{2,1,0:T(8,128)(2,1)S(1)}, bf16[8,8,256]{2,1,0:T(8,128)(2,1)S(1)}) custom-call(s32[1]{0:T(128)} %bitcast.region, s32[2,4]{1,0:T(2,128)S(1)} %copy-done, bf16[56,8,256]{2,1,0:T(8,128)(2,1)} %bitcast.17, f32[56,2,128]{2,1,0:T(2,128)} %bitcast.20, f32[56,2,128]{2,1,0:T(2,128)} %bitcast.23), custom_call_target="tpu_custom_call" | custom-call | tf_op jit(solution)/shard_map/pick/pallas_call | solution.py:357
  2.3 1.9 %collective-permute-start = (bf16[8,8,256]{2,1,0:T(8,128)(2,1)S(1)}, bf16[8,8,256]{2,1,0:T(8,128)(2,1)S(1)}, u32[]{:S(2)}, u32[]{:S(2)}) collective-permute-start(bf16[8,8,256]{2,1,0:T(8,128)(2,1)S(1)} %get-tuple-element.67), channel_id=1, source_target_pairs={{32,64},{64,32},{96,128},{128,96},{160,192},{192,160},{33,65},{65,... | collective-permute-start | bytes 98312 | tf_op jit(solution)/shard_map/ppermute | solution.py:317
  4.2 1.7 %collective-permute-start.1 = (bf16[8,8,256]{2,1,0:T(8,128)(2,1)S(1)}, bf16[8,8,256]{2,1,0:T(8,128)(2,1)S(1)}, u32[]{:S(2)}, u32[]{:S(2)}) collective-permute-start(bf16[8,8,256]{2,1,0:T(8,128)(2,1)S(1)} %get-tuple-element.68), channel_id=1, source_target_pairs={{0,32},{32,0},{64,96},{96,64},{128,160},{160,128},{192,224},{224,1... | collective-permute-start | bytes 98312 | tf_op jit(solution)/shard_map/ppermute | solution.py:317
  5.9 0.0 copy-start.2
  5.9 0.0 copy-start.1
  5.9 0.0 copy-start.3
  5.9 0.7 copy-done.2
  6.6 0.0 copy-done.1
  6.6 0.0 copy-done.3
  6.6 0.6 lists.1
  7.2 0.3 collective-permute-done
  7.5 0.0 collective-permute-done.1
  7.5 0.0 copy-done.6
  7.5 0.0 copy-done.7
  7.5 0.0 copy-done.8
  7.5 65.2 %conditional.1 = ((bf16[2,256,768]{2,1,0:T(8,128)(2,1)S(1)}, f32[2,8,768]{2,1,0:T(8,128)S(1)}, bf16[32,2,8,256]{3,2,1,0:T(8,128)(2,1)S(1)})) conditional(s32[]{:T(128)} %convert_element_type.3, (s32[1]{0:T(128)}, bf16[6,32,8,256]{3,2,1,0:T(8,128)(2,1)}, bf16[28,2,8,256]{3,2,1,0:T(8,128)(2,1)S(1)}, bf16[8,8,256]{2,1,0:T(8,128)(2,1)S(1)}, ...), branch_computations={%region_0.1_spmd, %region_1.2_spmd} | conditional | bytes 6291516 | solution.py:446
  7.5 1.2 %pack.3 = bf16[32,7,8,256]{3,2,1,0:T(8,128)(2,1)S(1)} custom-call(s32[1]{0:T(128)} %get-tuple-element.51.region.refs_1_, bf16[6,32,8,256]{3,2,1,0:T(8,128)(2,1)} %get-tuple-element.57.fields.refs_8_, bf16[28,2,8,256]{3,2,1,0:T(8,128)(2,1)S(1)} %get-tuple-element.58.blocks, bf16[8,8,256]{2,1,0:T(8,128)(2,1)S(1)} %get-tuple-element.55.across.refs_5_, ...), custom_call_target="tpu_custom_call" | custom-call | tf_op jit(solution)/shard_map/cond/branch_1_fun/pack/pallas_call | solution.py:384
  8.8 0.0 copy-start.5
  8.8 29.7 %all_to_all.32.refs_7_.refs_0_ = bf16[32,7,8,256]{3,2,1,0:T(8,128)(2,1)S(1)} all-to-all(bf16[32,7,8,256]{3,2,1,0:T(8,128)(2,1)S(1)} %pack.3), channel_id=1, replica_groups=mesh['region'=8,'member'=32] {'member'}, dimensions={0} | all-to-all | bytes 1835008 | tf_op jit(solution)/shard_map/cond/branch_1_fun/all_to_all | solution.py:321
  38.5 0.0 copy-done.5
  38.5 0.4 gram.3
  38.9 17.4 %all_to_all.33.entries.refs_1_ = bf16[32,3,8,256]{3,2,1,0:T(8,128)(2,1)S(1)} all-to-all(bf16[32,3,8,256]{3,2,1,0:T(8,128)(2,1)S(1)} %gram.3), channel_id=1, replica_groups=mesh['region'=8,'member'=32] {'member'}, dimensions={0} | all-to-all | bytes 786432 | tf_op jit(solution)/shard_map/cond/branch_1_fun/all_to_all | solution.py:321
  56.3 0.9 combine.3
  57.2 15.5 %all_to_all.34 = bf16[32,2,8,256]{3,2,1,0:T(8,128)(2,1)S(1)} all-to-all(bf16[32,2,8,256]{3,2,1,0:T(8,128)(2,1)S(1)} %get-tuple-element.61), channel_id=1, replica_groups=mesh['region'=8,'member'=32] {'member'}, dimensions={0} | all-to-all | bytes 524288 | tf_op jit(solution)/shard_map/cond/branch_1_fun/all_to_all | solution.py:321
  72.7 2.0 %mix.1 = bf16[32,6,8,256]{3,2,1,0:T(8,128)(2,1)S(1)} custom-call(bf16[32,2,8,256]{3,2,1,0:T(8,128)(2,1)S(1)} %get-tuple-element.69.entries, bf16[2,256,768]{2,1,0:T(8,128)(2,1)S(1)} %get-tuple-element.70.pert, f32[2,8,768]{2,1,0:T(8,128)S(1)} %get-tuple-element.71.centre), custom_call_target="tpu_custom_call" | custom-call | tf_op jit(solution)/shard_map/mix/pallas_call | solution.py:455
  74.7 22.0 %all_to_all.35.parts = bf16[32,6,8,256]{3,2,1,0:T(8,128)(2,1)S(1)} all-to-all(bf16[32,6,8,256]{3,2,1,0:T(8,128)(2,1)S(1)} %mix.1), channel_id=1, replica_groups=mesh['region'=8,'member'=32] {'member'}, dimensions={0} | all-to-all | bytes 1572864 | tf_op jit(solution)/shard_map/all_to_all | solution.py:321
  96.7 0.9 unpack.1
Async XLA Ops:
  0.0 0.7 copy-start
  0.0 7.5 %copy-start.6 = (bf16[8,14336]{1,0:T(8,128)(2,1)S(1)}, bf16[8,14336]{1,0:T(8,128)(2,1)}, u32[]{:S(2)}) copy-start(bf16[8,14336]{1,0:T(8,128)(2,1)} %param.11) | copy-start | bytes 688132
  0.7 6.8 %copy-start.7 = (f32[14336]{0:T(1024)S(1)}, f32[14336]{0:T(1024)}, u32[]{:S(2)}) copy-start(f32[14336]{0:T(1024)} %param.12) | copy-start | bytes 172036
  0.7 6.8 %copy-start.8 = (f32[14336]{0:T(1024)S(1)}, f32[14336]{0:T(1024)}, u32[]{:S(2)}) copy-start(f32[14336]{0:T(1024)} %param.13) | copy-start | bytes 172036
  2.3 5.2 %collective-permute-start = (bf16[8,8,256]{2,1,0:T(8,128)(2,1)S(1)}, bf16[8,8,256]{2,1,0:T(8,128)(2,1)S(1)}, u32[]{:S(2)}, u32[]{:S(2)}) collective-permute-start(bf16[8,8,256]{2,1,0:T(8,128)(2,1)S(1)} %get-tuple-element.67), channel_id=1, source_target_pairs={{32,64},{64,32},{96,128},{128,96},{160,192},{192,160},{33,65},{65,... | collective-permute-start | bytes 98312 | tf_op jit(solution)/shard_map/ppermute | solution.py:317
  4.2 3.3 %collective-permute-start.1 = (bf16[8,8,256]{2,1,0:T(8,128)(2,1)S(1)}, bf16[8,8,256]{2,1,0:T(8,128)(2,1)S(1)}, u32[]{:S(2)}, u32[]{:S(2)}) collective-permute-start(bf16[8,8,256]{2,1,0:T(8,128)(2,1)S(1)} %get-tuple-element.68), channel_id=1, source_target_pairs={{0,32},{32,0},{64,96},{96,64},{128,160},{160,128},{192,224},{224,1... | collective-permute-start | bytes 98312 | tf_op jit(solution)/shard_map/ppermute | solution.py:317
  5.9 0.7 copy-start.2
  5.9 0.7 copy-start.1
  5.9 0.7 copy-start.3
  8.8 29.7 %copy-start.5 = (bf16[6,32,8,256]{3,2,1,0:T(8,128)(2,1)S(1)}, bf16[6,32,8,256]{3,2,1,0:T(8,128)(2,1)}, u32[]{:S(2)}) copy-start(bf16[6,32,8,256]{3,2,1,0:T(8,128)(2,1)} %get-tuple-element.57.fields.refs_8_) | copy-start | bytes 2359300 | tf_op jit(solution)/shard_map/cond
